TPU v7x, 128 devices: a whole 4x4x4 slice. The times are simulated.
128 devices in a mesh: group: 4 (over z), dev: 32 (over x, y, core).
Axes of the slice: x: 4, y: 4, z: 4, core: 2. Of those that a mesh axis runs over, the one named last changes fastest.
Arguments:
- geometry: float32 [8192, 4, 256], P(('group', 'dev'))
- charges: float32 [8192, 16, 256], P(('group', 'dev')), may hold values from -6 to 6
- leaf_cluster_basis: float32 [8192, 32, 256], P(('group', 'dev')), may hold values from -1 to 1
- near_list: int32 [8192, 12], P(('group', 'dev')), may hold values from 0 to 8191, as said below
- near_count: int32 [8192], P(('group', 'dev')), may hold values from 1 to 12, as said below
- leaf_transfer: float32 [1024, 8, 32, 32], P(('group', 'dev')), may hold values from -0.375 to 0.375
- box_transfer: float32 [128, 8, 32, 32], P(('group', 'dev')), may hold values from -0.375 to 0.375
- box_far_list: int32 [1024, 16], P(('group', 'dev')), may hold values from 0 to 1023, as said below
- box_coupling: float32 [1024, 16, 32, 32], P(('group', 'dev')), may hold values from -0.25 to 0.25
- top_far_list: int32 [128, 16], P(('group', 'dev')), may hold values from 0 to 127, as said below
- top_coupling: float32 [128, 16, 32, 32], P(('group', 'dev')), may hold values from -0.25 to 0.25
Outputs:
- potential: float32 [8192, 16, 256], P(('group', 'dev'))
Inputs may be any that keep to these rules, and one draw needn't show every extreme that they name: `near_list`: row i holds distinct leaves whose index differs from i by at most 32; its first entry is i itself. `near_count`: leaf 0 uses all 12 slots. `box_far_list`: row b holds 16 distinct boxes other than b. `top_far_list`: row a holds 16 distinct upper boxes other than a.
All inputs are finite; a program needn't handle non-finite values.
Results may differ from a plain program's by a relative error of at most 0.0003.
Values sent between devices are 32-bit elements; how exact they have to be, the bound alone decides.
A program may use at most 64 MiB of HBM per device.

v0:
```python
import math

import jax
import jax.numpy as jnp
from jax import lax
from jax.sharding import PartitionSpec as P

NEAR_REACH = 32


SOFTENING = 0.0025
FOUR_PI = 4.0 * math.pi


def extended_2(shard, sides, width):
    for axis, dim in sides:
        size, length = (lax.axis_size(axis), shard.shape[dim])
        up = [(i, (i + 1) % size) for i in range(size - 1)]
        down = [(j, i) for i, j in up]
        last = lax.slice_in_dim(shard, length - width, length, axis=dim)
        first = lax.slice_in_dim(shard, 0, width, axis=dim)
        before = lax.ppermute(last, axis, up)
        after = lax.ppermute(first, axis, down)
        shard = jnp.concatenate([before, shard, after], axis=dim)
    return shard


def near_blocks(target, source):
    squared = jnp.zeros((target.shape[0], target.shape[2], source.shape[2]), jnp.float32)
    for comp in range(3):
        apart = target[:, comp, :, None] - source[:, comp, None, :]
        squared = squared + apart * apart
    kernel = source[:, 3, None, :] / (FOUR_PI * jnp.sqrt(squared + SOFTENING))
    return jnp.einsum("npq,nsq->nsp", kernel, source[:, 4:, :], precision=lax.Precision.HIGHEST)


def on_device(
    geometry,
    charges,
    leaf_cluster_basis,
    near_list,
    near_count,
    leaf_transfer,
    box_transfer,
    box_far_list,
    box_coupling,
    top_far_list,
    top_coupling,
):
    leaf_dev, rhs_count, panels = charges.shape
    rank_width = leaf_cluster_basis.shape[1]
    slots_total = near_list.shape[1]
    reach_rows = NEAR_REACH
    stacked = jnp.concatenate([geometry, charges], axis=1)
    extended = extended_2(stacked, ((("group", "dev"), 0),), reach_rows)
    offset_rows = lax.axis_index(("group", "dev")) * leaf_dev - reach_rows
    local_lists = near_list - offset_rows
    started = jnp.zeros((leaf_dev, rhs_count, panels), jnp.float32)

    def slot_term(index_of_slot, running):
        source = jnp.take(extended, local_lists[:, index_of_slot], axis=0)
        block_group = near_blocks(geometry, source)
        return running + jnp.where((index_of_slot < near_count)[:, None, None], block_group, 0.0)

    nearby_panels = lax.fori_loop(0, slots_total, slot_term, started)
    finest_level = lax.Precision.HIGHEST
    box_dev = leaf_dev // 8
    top_dev = leaf_dev // 64
    leaf_moment_values = jnp.einsum(
        "gvx,gfx->gfv", leaf_cluster_basis, charges, precision=finest_level
    )
    box_moments = jnp.einsum(
        "bcsr,bcrt->bst",
        leaf_moment_values.reshape(box_dev, 8, rhs_count, rank_width),
        leaf_transfer,
        precision=finest_level,
    )
    top_moments = jnp.einsum(
        "acsr,acrt->ast",
        box_moments.reshape(top_dev, 8, rhs_count, rank_width),
        box_transfer,
        precision=finest_level,
    )
    everyone = lax.all_gather(box_moments, ("group", "dev"), axis=0, tiled=True)
    picked = jnp.take(everyone, box_far_list, axis=0)
    all_tops = lax.all_gather(top_moments, ("group", "dev"), axis=0, tiled=True)
    top_picked = jnp.take(all_tops, top_far_list, axis=0)
    top_local = jnp.einsum("afsr,afrt->ast", top_picked, top_coupling, precision=finest_level)
    box_far = jnp.einsum("bfsu,bfur->bsr", picked, box_coupling, precision=finest_level)
    box_down = jnp.einsum(
        "ast,acrt->acsr", top_local, box_transfer, precision=finest_level
    ).reshape(box_dev, rhs_count, rank_width)
    box_local = box_far + box_down
    leaf_local_expansion = jnp.einsum(
        "bst,bcrt->bcsr", box_local, leaf_transfer, precision=finest_level
    ).reshape(leaf_dev, rhs_count, rank_width)
    return nearby_panels + jnp.einsum(
        "hmw,hwq->hmq", leaf_local_expansion, leaf_cluster_basis, precision=finest_level
    )


def solution(mesh):
    in_specs = (
        P(("group", "dev"), None, None),
        P(("group", "dev"), None, None),
        P(("group", "dev"), None, None),
        P(("group", "dev"), None),
        P(("group", "dev")),
        P(("group", "dev"), None, None, None),
        P(("group", "dev"), None, None, None),
        P(("group", "dev"), None),
        P(("group", "dev"), None, None, None),
        P(("group", "dev"), None),
        P(("group", "dev"), None, None, None),
    )
    out_specs = P(("group", "dev"), None, None)
    return jax.shard_map(
        on_device, mesh=mesh, in_specs=in_specs, out_specs=out_specs, check_vma=False
    )
```

profile of v0, /device:TPU:1, one launch (start us, length us, event | category | flops | bytes accessed | tf_op | source)
XLA Modules:
  0.0 567.3 jit_solution(1215687572607000891)
XLA Ops:
  18.1 4.6 collective-permute-start
  27.0 45.7 %all-gather = f32[2048,32]{1,0:T(8,128)} all-gather(f32[16,32]{1,0:T(8,128)S(1)} %convolution_bitcast_fusion.3), channel_id=2, replica_groups=mesh['group'=4,'dev'=32] {'group','dev'}, dimensions={0}, use_global_device_ids=true | all-gather | bytes 264192 | tf_op jit(solution)/shard_map/all_gather | solution.py:86
  82.2 461.1 %while.14 = (s32[]{:T(128)}, f32[64,16,256]{2,1,0:T(8,128)}, s32[64]{0:T(128)S(1)}, s32[64,12]{0,1:T(8,128)S(1)}, f32[128,20,256]{2,1,0:T(8,128)}, /*index=5*/f32[64,4,256]{2,0,1:T(8,128)S(1)}, s32[]{:T(128)}, s32[]{:T(128)}) while((s32[]{:T(128)}, f32[64,16,256]{2,1,0:T(8,128)}, s32[64]{0:T(128)S(1)}, s32[64,12]{0,1:T(8,128)S(1)}, ...), condition=%wide.region_1.0_spmd.clone, body=%wide.region_0.1_spmd.clone.sunk | while | flops 852559296 | bytes 18684008 | solution.py:65
  82.5 4.1 gather_fusion
  88.4 31.7 %fusion.52 = f32[64,16,256]{2,1,0:T(8,128)S(1)} fusion(f32[64,256]{1,0:T(8,128)S(1)} %get-tuple-element.231, f32[64,256]{1,0:T(8,128)S(1)} %get-tuple-element.232, f32[64,256]{1,0:T(8,128)S(1)} %get-tuple-element.233, f32[64,256]{1,0:T(8,128)S(1)} %get-tuple-element.234, f32[64,256]{1,0:T(8,128)S(1)} %get-tuple-element.237, ...), kind=kOutput, calls=%fused_computation.15.clone.1 | convolution fusion | flops 852230144 | bytes 3604993 | tf_op jit(solution)/shard_map/while/body/eval_jaxpr/npq,nsq->nsp/dot_general | solution.py:34
  121.1 3.8 gather_fusion
  126.8 31.7 %fusion.52 = f32[64,16,256]{2,1,0:T(8,128)S(1)} fusion(f32[64,256]{1,0:T(8,128)S(1)} %get-tuple-element.231, f32[64,256]{1,0:T(8,128)S(1)} %get-tuple-element.232, f32[64,256]{1,0:T(8,128)S(1)} %get-tuple-element.233, f32[64,256]{1,0:T(8,128)S(1)} %get-tuple-element.234, f32[64,256]{1,0:T(8,128)S(1)} %get-tuple-element.237, ...), kind=kOutput, calls=%fused_computation.15.clone.1 | convolution fusion | flops 852230144 | bytes 3604993 | tf_op jit(solution)/shard_map/while/body/eval_jaxpr/npq,nsq->nsp/dot_general | solution.py:34
  159.5 3.8 gather_fusion
  165.2 31.7 %fusion.52 = f32[64,16,256]{2,1,0:T(8,128)S(1)} fusion(f32[64,256]{1,0:T(8,128)S(1)} %get-tuple-element.231, f32[64,256]{1,0:T(8,128)S(1)} %get-tuple-element.232, f32[64,256]{1,0:T(8,128)S(1)} %get-tuple-element.233, f32[64,256]{1,0:T(8,128)S(1)} %get-tuple-element.234, f32[64,256]{1,0:T(8,128)S(1)} %get-tuple-element.237, ...), kind=kOutput, calls=%fused_computation.15.clone.1 | convolution fusion | flops 852230144 | bytes 3604993 | tf_op jit(solution)/shard_map/while/body/eval_jaxpr/npq,nsq->nsp/dot_general | solution.py:34
  197.9 3.8 gather_fusion
  203.6 31.7 %fusion.52 = f32[64,16,256]{2,1,0:T(8,128)S(1)} fusion(f32[64,256]{1,0:T(8,128)S(1)} %get-tuple-element.231, f32[64,256]{1,0:T(8,128)S(1)} %get-tuple-element.232, f32[64,256]{1,0:T(8,128)S(1)} %get-tuple-element.233, f32[64,256]{1,0:T(8,128)S(1)} %get-tuple-element.234, f32[64,256]{1,0:T(8,128)S(1)} %get-tuple-element.237, ...), kind=kOutput, calls=%fused_computation.15.clone.1 | convolution fusion | flops 852230144 | bytes 3604993 | tf_op jit(solution)/shard_map/while/body/eval_jaxpr/npq,nsq->nsp/dot_general | solution.py:34
  236.3 3.8 gather_fusion
  241.9 31.7 %fusion.52 = f32[64,16,256]{2,1,0:T(8,128)S(1)} fusion(f32[64,256]{1,0:T(8,128)S(1)} %get-tuple-element.231, f32[64,256]{1,0:T(8,128)S(1)} %get-tuple-element.232, f32[64,256]{1,0:T(8,128)S(1)} %get-tuple-element.233, f32[64,256]{1,0:T(8,128)S(1)} %get-tuple-element.234, f32[64,256]{1,0:T(8,128)S(1)} %get-tuple-element.237, ...), kind=kOutput, calls=%fused_computation.15.clone.1 | convolution fusion | flops 852230144 | bytes 3604993 | tf_op jit(solution)/shard_map/while/body/eval_jaxpr/npq,nsq->nsp/dot_general | solution.py:34
  274.6 3.8 gather_fusion
  280.3 31.7 %fusion.52 = f32[64,16,256]{2,1,0:T(8,128)S(1)} fusion(f32[64,256]{1,0:T(8,128)S(1)} %get-tuple-element.231, f32[64,256]{1,0:T(8,128)S(1)} %get-tuple-element.232, f32[64,256]{1,0:T(8,128)S(1)} %get-tuple-element.233, f32[64,256]{1,0:T(8,128)S(1)} %get-tuple-element.234, f32[64,256]{1,0:T(8,128)S(1)} %get-tuple-element.237, ...), kind=kOutput, calls=%fused_computation.15.clone.1 | convolution fusion | flops 852230144 | bytes 3604993 | tf_op jit(solution)/shard_map/while/body/eval_jaxpr/npq,nsq->nsp/dot_general | solution.py:34
  318.7 31.7 %fusion.52 = f32[64,16,256]{2,1,0:T(8,128)S(1)} fusion(f32[64,256]{1,0:T(8,128)S(1)} %get-tuple-element.231, f32[64,256]{1,0:T(8,128)S(1)} %get-tuple-element.232, f32[64,256]{1,0:T(8,128)S(1)} %get-tuple-element.233, f32[64,256]{1,0:T(8,128)S(1)} %get-tuple-element.234, f32[64,256]{1,0:T(8,128)S(1)} %get-tuple-element.237, ...), kind=kOutput, calls=%fused_computation.15.clone.1 | convolution fusion | flops 852230144 | bytes 3604993 | tf_op jit(solution)/shard_map/while/body/eval_jaxpr/npq,nsq->nsp/dot_general | solution.py:34
  357.1 31.7 %fusion.52 = f32[64,16,256]{2,1,0:T(8,128)S(1)} fusion(f32[64,256]{1,0:T(8,128)S(1)} %get-tuple-element.231, f32[64,256]{1,0:T(8,128)S(1)} %get-tuple-element.232, f32[64,256]{1,0:T(8,128)S(1)} %get-tuple-element.233, f32[64,256]{1,0:T(8,128)S(1)} %get-tuple-element.234, f32[64,256]{1,0:T(8,128)S(1)} %get-tuple-element.237, ...), kind=kOutput, calls=%fused_computation.15.clone.1 | convolution fusion | flops 852230144 | bytes 3604993 | tf_op jit(solution)/shard_map/while/body/eval_jaxpr/npq,nsq->nsp/dot_general | solution.py:34
  395.5 31.7 %fusion.52 = f32[64,16,256]{2,1,0:T(8,128)S(1)} fusion(f32[64,256]{1,0:T(8,128)S(1)} %get-tuple-element.231, f32[64,256]{1,0:T(8,128)S(1)} %get-tuple-element.232, f32[64,256]{1,0:T(8,128)S(1)} %get-tuple-element.233, f32[64,256]{1,0:T(8,128)S(1)} %get-tuple-element.234, f32[64,256]{1,0:T(8,128)S(1)} %get-tuple-element.237, ...), kind=kOutput, calls=%fused_computation.15.clone.1 | convolution fusion | flops 852230144 | bytes 3604993 | tf_op jit(solution)/shard_map/while/body/eval_jaxpr/npq,nsq->nsp/dot_general | solution.py:34
  433.9 31.7 %fusion.52 = f32[64,16,256]{2,1,0:T(8,128)S(1)} fusion(f32[64,256]{1,0:T(8,128)S(1)} %get-tuple-element.231, f32[64,256]{1,0:T(8,128)S(1)} %get-tuple-element.232, f32[64,256]{1,0:T(8,128)S(1)} %get-tuple-element.233, f32[64,256]{1,0:T(8,128)S(1)} %get-tuple-element.234, f32[64,256]{1,0:T(8,128)S(1)} %get-tuple-element.237, ...), kind=kOutput, calls=%fused_computation.15.clone.1 | convolution fusion | flops 852230144 | bytes 3604993 | tf_op jit(solution)/shard_map/while/body/eval_jaxpr/npq,nsq->nsp/dot_general | solution.py:34
  472.2 31.7 %fusion.52 = f32[64,16,256]{2,1,0:T(8,128)S(1)} fusion(f32[64,256]{1,0:T(8,128)S(1)} %get-tuple-element.231, f32[64,256]{1,0:T(8,128)S(1)} %get-tuple-element.232, f32[64,256]{1,0:T(8,128)S(1)} %get-tuple-element.233, f32[64,256]{1,0:T(8,128)S(1)} %get-tuple-element.234, f32[64,256]{1,0:T(8,128)S(1)} %get-tuple-element.237, ...), kind=kOutput, calls=%fused_computation.15.clone.1 | convolution fusion | flops 852230144 | bytes 3604993 | tf_op jit(solution)/shard_map/while/body/eval_jaxpr/npq,nsq->nsp/dot_general | solution.py:34
  510.6 31.7 %fusion.52 = f32[64,16,256]{2,1,0:T(8,128)S(1)} fusion(f32[64,256]{1,0:T(8,128)S(1)} %get-tuple-element.231, f32[64,256]{1,0:T(8,128)S(1)} %get-tuple-element.232, f32[64,256]{1,0:T(8,128)S(1)} %get-tuple-element.233, f32[64,256]{1,0:T(8,128)S(1)} %get-tuple-element.234, f32[64,256]{1,0:T(8,128)S(1)} %get-tuple-element.237, ...), kind=kOutput, calls=%fused_computation.15.clone.1 | convolution fusion | flops 852230144 | bytes 3604993 | tf_op jit(solution)/shard_map/while/body/eval_jaxpr/npq,nsq->nsp/dot_general | solution.py:34
  543.3 5.2 gather_fusion.1
  548.5 4.8 convolution_bitcast_fusion.2
  553.9 4.2 fusion.34
  (206 shorter events, 85.4 us)
Async XLA Ops:
  6.5 4.6 copy-start.2
  6.5 536.7 %all-gather.3.cloned.1.call-start = ((), (), s32[]{:S(2)}) async-start(), calls=%async_computation | async-start | bytes 8454144 | tf_op jit(solution)/shard_map/all_gather | solution.py:84
  13.3 11.3 %copy-start.11 = (s32[8,16]{1,0:T(8,128)S(1)}, s32[8,16]{1,0:T(8,128)}, u32[]{:S(2)}) copy-start(s32[8,16]{1,0:T(8,128)} %param.20) | copy-start | bytes 1540
  13.3 11.9 %copy-start.14 = (s32[1,16]{1,0:T(1,128)S(1)}, s32[1,16]{1,0:T(1,128)}, u32[]{:S(2)}) copy-start(s32[1,16]{1,0:T(1,128)} %param.22) | copy-start | bytes 196
  13.3 12.5 %copy-start.7 = (f32[8,16,32]{2,1,0:T(8,128)S(1)}, f32[8,16,32]{2,1,0:T(8,128)}, u32[]{:S(2)}) copy-start(f32[8,16,32]{2,1,0:T(8,128)} %convolution_bitcast_fusion) | copy-start | bytes 49156
  16.9 58.3 %copy-start.12 = (s32[64,12]{0,1:T(8,128)S(1)}, s32[64,12]{0,1:T(8,128)}, u32[]{:S(2)}) copy-start(s32[64,12]{0,1:T(8,128)} %param.16) | copy-start | bytes 9220
  18.1 59.3 %collective-permute-start = (f32[32,20,256]{2,0,1:T(8,128)}, f32[32,20,256]{2,0,1:T(8,128)}, u32[]{:S(2)}, u32[]{:S(2)}) collective-permute-start(f32[32,20,256]{2,0,1:T(8,128)} %get-tuple-element.173), channel_id=1, source_target_pairs={{0,1},{1,2},{2,3},{3,4},{4,5},{5,6},{6,7},{7,8},{8,9},{9,10},{10,1... | collective-permute-start | bytes 1966088 | tf_op jit(solution)/shard_map/ppermute | solution.py:22
  22.7 54.7 %collective-permute-start.1 = (f32[32,20,256]{2,0,1:T(8,128)}, f32[32,20,256]{2,0,1:T(8,128)}, u32[]{:S(2)}, u32[]{:S(2)}) collective-permute-start(f32[32,20,256]{2,0,1:T(8,128)} %get-tuple-element.174), channel_id=1, source_target_pairs={{1,0},{2,1},{3,2},{4,3},{5,4},{6,5},{7,6},{8,7},{9,8},{10,9},{11,1... | collective-permute-start | bytes 1966088 | tf_op jit(solution)/shard_map/ppermute | solution.py:23
  78.9 3.2 copy-start.1
  78.9 3.2 copy-start.15
  82.2 461.1 %copy-start.10 = (s32[1024]{0:T(1024)S(1)}, s32[1024]{0:T(1024)}, u32[]{:S(2)}) copy-start(s32[1024]{0:T(1024)} %pad_clamp_fusion.2) | copy-start | bytes 12292
  82.2 466.3 %copy-start.13 = (pred[8,16]{1,0:T(8,128)(4,1)S(1)}, pred[8,16]{1,0:T(8,128)(4,1)}, u32[]{:S(2)}) copy-start(pred[8,16]{1,0:T(8,128)(4,1)} %compare_and_fusion) | copy-start | bytes 388
  86.5 1.9 copy-start.4
  124.9 1.9 copy-start.4
  163.3 1.9 copy-start.4
  201.7 1.9 copy-start.4
  240.0 1.9 copy-start.4
  278.4 1.9 copy-start.4
  393.6 1.9 copy-start.4
  431.9 1.9 copy-start.4
  543.3 10.0 %copy-start.8 = (f32[1,8,32,32]{3,2,1,0:T(8,128)S(1)}, f32[1,8,32,32]{3,2,1,0:T(8,128)}, u32[]{:S(2)}) copy-start(f32[1,8,32,32]{3,2,1,0:T(8,128)} %param.19) | copy-start | bytes 98308
  543.3 10.0 %copy-start.9 = (f32[16,32,1]{1,0,2:T(8,128)S(1)}, f32[16,32,1]{1,0,2:T(8,128)}, u32[]{:S(2)}) copy-start(f32[16,32,1]{1,0,2:T(8,128)} %fusion.20) | copy-start | bytes 6148
  543.3 10.6 %copy-start.3 = (f32[8,8,32,32]{3,2,1,0:T(8,128)S(1)}, f32[8,8,32,32]{3,2,1,0:T(8,128)}, u32[]{:S(2)}) copy-start(f32[8,8,32,32]{3,2,1,0:T(8,128)} %param.18) | copy-start | bytes 786436
  553.9 5.4 copy-start.6
  (17 other events, 20.9 us)
Sparse Core Ops, SparseCore 0:
  13.4 77.3 all-gather.2
where the time goes:
time: 569 us; the launch traced here: 567 us
  matrix products  399 us (70%)
  local copies, waits for them, and re-layouts  76.5 us (13%)
  blocking collectives  45.7 us (8%)
  other arithmetic  24.9 us (4%)
  between operations  13.6 us (2%)
  starting transfers between devices  6.51 us (1%)
    dot_general x12, matrix products, near_blocks(): jnp.einsum('npq,nsq->nsp', kernel, source[:, 4:, :], precision=lax.Precis...  380 us
    all_gather x1, blocking collectives, on_device(): all_tops = lax.all_gather(top_moments, ('group', 'dev'), axis=0, tiled=True)  45.7 us
    gather x12, local copies, waits for them, and re-layouts, slot_term(): source = jnp.take(extended, local_lists[:, index_of_slot], axis=0)  45.6 us
    select_n x12, other arithmetic, slot_term(): source = jnp.take(extended, local_lists[:, index_of_slot], axis=0)  20 us
    while x72, local copies, waits for them, and re-layouts  11.9 us
  transfers between devices with their start and end apart: 3, of which 0 were waited for; matrix products, arithmetic and copies ran while one was open for 82% of the time, Pallas kernels for 0%

commit v1 on v0

v1 whole, which is shorter than its diff:
```python
import functools
import math

import jax
import jax.numpy as jnp
from jax import lax
from jax.experimental import pallas as pl
from jax.experimental.pallas import tpu as pltpu
from jax.sharding import PartitionSpec as P

SOFTENING = 0.0025
FOUR_PI = 4.0 * math.pi
AXES = ("group", "dev")

LEAF = 256
RANK = 32
RHS = 16
NEAR = 12
FAR = 16
REACH = 32
OWN = 64
WIDE = OWN + 2 * REACH
UNROLL = 12
FEATURES = 48
EXTENT = 8.0

f32 = jnp.float32
bf16 = jnp.bfloat16
NN = (((1,), (0,)), ((), ()))
NT = (((1,), (1,)), ((), ()))


def dot(a, b, dims):
    return lax.dot_general(a, b, dims, preferred_element_type=f32)


def halves(v):
    hi = v.astype(bf16)
    return hi, (v - hi.astype(f32)).astype(bf16)


def thirds(v):
    a = v.astype(bf16).astype(f32)
    b = (v - a).astype(bf16).astype(f32)
    return a, b, v - a - b


def dot3(a, b, dims):
    ah, al = halves(a)
    bh, bl = halves(b)
    rows = a.shape[0]
    both = dot(jnp.concatenate([ah, al], axis=0), bh, dims)
    return both[:rows] + both[rows:] + dot(ah, bl, dims)


def upward_kernel(charges, basis, leaf_transfer, box_transfer, out, moments):
    box = pl.program_id(0)
    parts = [dot3(charges[c], basis[c], NT) for c in range(8)]
    leaf_moments = jnp.concatenate(parts, axis=1)
    moments[box] = dot3(leaf_moments, leaf_transfer[...].reshape(8 * RANK, RANK), NN)

    @pl.when(box == 7)
    def _():
        boxes = jnp.concatenate([moments[b] for b in range(8)], axis=1)
        top = dot3(boxes, box_transfer[...].reshape(8 * RANK, RANK), NN)
        out[0, :, : 8 * RANK] = boxes
        out[0, :, 8 * RANK :] = jnp.concatenate([top, jnp.zeros((RHS, 128 - RANK), f32)], axis=1)


def upward(charges, basis, leaf_transfer, box_transfer):
    return pl.pallas_call(
        upward_kernel,
        grid=(8,),
        out_shape=jax.ShapeDtypeStruct((1, RHS, 8 * RANK + 128), f32),
        in_specs=[
            pl.BlockSpec((8, RHS, LEAF), lambda b: (b, 0, 0)),
            pl.BlockSpec((8, RANK, LEAF), lambda b: (b, 0, 0)),
            pl.BlockSpec((1, 8, RANK, RANK), lambda b: (b, 0, 0, 0)),
            pl.BlockSpec((1, 8, RANK, RANK), lambda b: (0, 0, 0, 0)),
        ],
        out_specs=pl.BlockSpec((1, RHS, 8 * RANK + 128), lambda b: (0, 0, 0)),
        scratch_shapes=[pltpu.VMEM((8, RHS, RANK), f32)],
        compiler_params=pltpu.CompilerParams(vmem_limit_bytes=16 * 2**20),
        cost_estimate=pl.CostEstimate(flops=10**8, bytes_accessed=5 * 10**6, transcendentals=0),
        name="upward",
    )(charges, basis, leaf_transfer, box_transfer)


def near_kernel(
    place, near_list, near_count, geometry, geo_before, geo_after, charges, ch_before, ch_after,
    out, geo, source, source_rows, target_rows, block_hi, block_lo, total, extent,
):
    me = place[0]
    offset = me * OWN - REACH
    geo[0:REACH] = geo_before[...]
    geo[REACH : REACH + OWN] = geometry[...]
    geo[REACH + OWN :] = geo_after[...]
    centre = jnp.broadcast_to(jnp.mean(geometry[OWN // 2], axis=1, keepdims=True), (4, LEAF))
    one = jnp.ones((1, LEAF), f32)
    rest = jnp.zeros((3, LEAF), f32)

    def squared_norm(v):
        return v[0:1] * v[0:1] + v[1:2] * v[1:2] + v[2:3] * v[2:3]

    def weigh(part, start):
        def leaf(n, carry):
            area = geo[start + n][3:4] * (1.0 / FOUR_PI)
            hi, lo = halves(part[n] * area)
            source[start + n] = jnp.concatenate([hi, lo], axis=0)
            return carry

        lax.fori_loop(0, part.shape[0], leaf, 0, unroll=8)

    weigh(ch_before, 0)
    weigh(charges, REACH)
    weigh(ch_after, REACH + OWN)

    def target(n, largest):
        v = geo[n + REACH] - centre
        norm = squared_norm(v)
        a, b, c = thirds(jnp.concatenate([v[0:3], one, norm + SOFTENING, rest], axis=0))
        target_rows[n] = jnp.concatenate([a, a, b, b, a, c], axis=0).astype(bf16)
        total[n] = jnp.zeros((RHS, LEAF), f32)
        return jnp.maximum(largest, norm)

    def neighbour(n, largest):
        v = geo[n] - centre
        norm = squared_norm(v)
        a, b, c = thirds(jnp.concatenate([-2.0 * v[0:3], norm, one, rest], axis=0))
        source_rows[n, :, :FEATURES] = jnp.concatenate([a, b, a, b, c, a], axis=0).astype(bf16).T
        leaf = offset + n
        held = (leaf >= 0) & (leaf < place[1])
        return jnp.maximum(largest, jnp.where(held, norm, 0.0))

    nothing = jnp.zeros((1, LEAF), f32)
    targets = lax.fori_loop(0, OWN, target, nothing, unroll=8)
    sources = lax.fori_loop(0, WIDE, neighbour, nothing, unroll=8)
    total[OWN] = jnp.zeros((RHS, LEAF), f32)
    extent[0] = jnp.max(targets) + jnp.max(sources)
    compact = extent[0] <= EXTENT

    @pl.when(compact)
    def _():
        pairs = lax.fori_loop(0, OWN, lambda n, s: s + near_count[n], 0)

        def after(leaf, slot):
            row = jnp.minimum(leaf, OWN - 1)
            more = slot + 1 < near_count[row]
            return jnp.where(more, leaf, jnp.minimum(leaf + 1, OWN)), jnp.where(more, slot + 1, 0)

        def fill(u, leaf, slot):
            row = jnp.minimum(leaf, OWN - 1)
            j = near_list[row, slot] - offset
            for q in range(0, LEAF, 128):
                entries = lax.rsqrt(dot(source_rows[j, q : q + 128, :FEATURES], target_rows[row], NN))
                hi, lo = halves(entries)
                block_hi[u, q : q + 128] = hi
                block_lo[u, q : q + 128] = lo
            return j

        def use(u, leaf, j):
            both = source[j]
            r = dot(both, block_hi[u], NN)
            total[leaf] = total[leaf] + (r[:RHS] + r[RHS:] + dot(both[:RHS], block_lo[u], NN))

        def round_of(state, use_old):
            leaf, slot = state[0], state[1]
            new = []
            for u in range(UNROLL):
                if use_old:
                    use(u, state[2 + 2 * u], state[3 + 2 * u])
                new += [leaf, fill(u, leaf, slot)]
                leaf, slot = after(leaf, slot)
            return (leaf, slot, *new)

        start = round_of((jnp.int32(0), jnp.int32(0)), False)
        lax.fori_loop(0, (pairs + UNROLL - 1) // UNROLL, lambda t, s: round_of(s, True), start)

    @pl.when(jnp.logical_not(compact))
    def _():
        def leaf_sum(n, carry):
            columns = geo[n + REACH].T

            def slot_sum(k, running):
                j = near_list[n, k] - offset
                v = geo[j]
                both = source[j]
                parts = []
                for p in range(0, LEAF, 128):
                    squared = jnp.full((128, LEAF), SOFTENING, f32)
                    for comp in range(3):
                        apart = columns[p : p + 128, comp : comp + 1] - v[comp : comp + 1]
                        squared = squared + apart * apart
                    hi, lo = halves(lax.rsqrt(squared))
                    r = dot(both, hi, NT)
                    parts.append(r[:RHS] + r[RHS:] + dot(both[:RHS], lo, NT))
                return running + jnp.concatenate(parts, axis=1)

            total[n] = lax.fori_loop(0, near_count[n], slot_sum, jnp.zeros((RHS, LEAF), f32))
            return carry

        lax.fori_loop(0, OWN, leaf_sum, 0)

    out[...] = total[0:OWN]


def near_field(place, near_list, near_count, *arrays):
    smem = pl.BlockSpec(memory_space=pltpu.SMEM)
    vmem = pl.BlockSpec(memory_space=pltpu.VMEM)
    return pl.pallas_call(
        near_kernel,
        out_shape=jax.ShapeDtypeStruct((OWN, RHS, LEAF), f32),
        in_specs=[smem] * 3 + [vmem] * 6,
        out_specs=vmem,
        scratch_shapes=[
            pltpu.VMEM((WIDE, 4, LEAF), f32),
            pltpu.VMEM((WIDE, 2 * RHS, LEAF), bf16),
            pltpu.VMEM((WIDE, LEAF, 128), bf16),
            pltpu.VMEM((OWN, FEATURES, LEAF), bf16),
            pltpu.VMEM((UNROLL, LEAF, LEAF), bf16),
            pltpu.VMEM((UNROLL, LEAF, LEAF), bf16),
            pltpu.VMEM((OWN + 1, RHS, LEAF), f32),
            pltpu.SMEM((1,), f32),
        ],
        compiler_params=pltpu.CompilerParams(vmem_limit_bytes=40 * 2**20),
        cost_estimate=pl.CostEstimate(flops=2 * 10**10, bytes_accessed=4 * 10**6, transcendentals=5 * 10**7),
        name="near_field",
    )(place, near_list, near_count, *arrays)


def downward_kernel(
    box_far_list, top_far_list, gathered, top_coupling, box_transfer, box_coupling, leaf_transfer, basis, near,
    out, box_down,
):
    box = pl.program_id(0)

    @pl.when(box == 0)
    def _():
        top_local = jnp.zeros((RHS, RANK), f32)
        for f in range(FAR):
            top = gathered[top_far_list[0, f], :, 8 * RANK : 8 * RANK + RANK]
            top_local = top_local + dot3(top, top_coupling[0, f], NN)
        down = dot3(top_local, box_transfer[...].reshape(8 * RANK, RANK), NT)
        for b in range(8):
            box_down[b] = down[:, b * RANK : (b + 1) * RANK]

    local = box_down[box]
    for f in range(FAR):
        far = box_far_list[box, f]
        lane = (far % 8) * RANK
        base = pl.multiple_of((lane // 128) * 128, 128)
        tile = gathered[far // 8, :, pl.ds(base, 128)]
        tile = pltpu.roll(tile, (128 - lane % 128) % 128, 1)
        local = local + dot3(tile[:, :RANK], box_coupling[0, f], NN)
    leaves = dot3(local, leaf_transfer[...].reshape(8 * RANK, RANK), NT)
    for c in range(8):
        out[c] = near[c] + dot3(leaves[:, c * RANK : (c + 1) * RANK], basis[c], NN)


def downward(box_far_list, top_far_list, gathered, top_coupling, box_transfer, box_coupling, leaf_transfer, basis, near):
    smem = pl.BlockSpec(memory_space=pltpu.SMEM)
    vmem = pl.BlockSpec(memory_space=pltpu.VMEM)
    return pl.pallas_call(
        downward_kernel,
        grid=(8,),
        out_shape=jax.ShapeDtypeStruct((OWN, RHS, LEAF), f32),
        in_specs=[
            smem,
            smem,
            vmem,
            vmem,
            vmem,
            pl.BlockSpec((1, FAR, RANK, RANK), lambda b: (b, 0, 0, 0)),
            pl.BlockSpec((1, 8, RANK, RANK), lambda b: (b, 0, 0, 0)),
            pl.BlockSpec((8, RANK, LEAF), lambda b: (b, 0, 0)),
            pl.BlockSpec((8, RHS, LEAF), lambda b: (b, 0, 0)),
        ],
        out_specs=pl.BlockSpec((8, RHS, LEAF), lambda b: (b, 0, 0)),
        scratch_shapes=[pltpu.VMEM((8, RHS, RANK), f32)],
        compiler_params=pltpu.CompilerParams(vmem_limit_bytes=24 * 2**20),
        name="downward",
    )(box_far_list, top_far_list, gathered, top_coupling, box_transfer, box_coupling, leaf_transfer, basis, near)


def on_device(
    geometry,
    charges,
    leaf_cluster_basis,
    near_list,
    near_count,
    leaf_transfer,
    box_transfer,
    box_far_list,
    box_coupling,
    top_far_list,
    top_coupling,
):
    size = lax.axis_size(AXES)
    up = [(i, i + 1) for i in range(size - 1)]
    down = [(i + 1, i) for i in range(size - 1)]
    geo_before = lax.ppermute(geometry[OWN - REACH :], AXES, up)
    geo_after = lax.ppermute(geometry[:REACH], AXES, down)
    ch_before = lax.ppermute(charges[OWN - REACH :], AXES, up)
    ch_after = lax.ppermute(charges[:REACH], AXES, down)
    moments = upward(charges, leaf_cluster_basis, leaf_transfer, box_transfer)
    gathered = lax.all_gather(moments, AXES, axis=0, tiled=True)
    place = jnp.stack([lax.axis_index(AXES), jnp.int32(size * OWN)]).astype(jnp.int32)
    near = near_field(
        place, near_list, near_count, geometry, geo_before, geo_after, charges, ch_before, ch_after
    )
    return downward(
        box_far_list, top_far_list, gathered, top_coupling, box_transfer, box_coupling, leaf_transfer,
        leaf_cluster_basis, near,
    )


def solution(mesh):
    wide = P(AXES)
    return jax.shard_map(on_device, mesh=mesh, in_specs=(wide,) * 11, out_specs=wide, check_vma=False)
```

time: 569 us -> 106 us (0.19)
  matrix products: 399 us -> 0 us
  local copies, waits for them, and re-layouts: 76.5 us -> 19.1 us
  blocking collectives: 45.7 us -> 0 us
  Pallas kernels: 0 us -> 38.7 us
  other arithmetic: 24.9 us -> 0.07 us
  waiting for transfers between devices: 0.03 us -> 22.4 us
    dot_general x20 -> x0, matrix products: 399 us -> none  [the longest x12 380 us: near_blocks(): jnp.einsum('npq,nsq->nsp', kernel, source[:, 4:, :], precision=lax.Precis...]
    gather x14 -> x0, local copies, waits for them, and re-layouts: 52.6 us -> none  [the longest x12 45.6 us: slot_term(): source = jnp.take(extended, local_lists[:, index_of_slot], axis=0)]
    all_gather x1 -> x0, blocking collectives: 45.7 us -> none  [on_device(): all_tops = lax.all_gather(top_moments, ('group', 'dev'), axis=0, tiled=True)]
    pallas_call x0 -> x3, Pallas kernels: none -> 38.7 us  [the longest x1 25.6 us: near_field(): pl.pallas_call(near_kernel, out_shape=jax.ShapeDtypeStruct((OWN, RHS, LEA...]
    select_n x13 -> x0, other arithmetic: 20 us -> none  [the longest x12 20 us: slot_term(): source = jnp.take(extended, local_lists[:, index_of_slot], axis=0)]
    all_gather x1, waiting for transfers between devices: 0.01 us -> 19 us  [on_device(): gathered = lax.all_gather(moments, AXES, axis=0, tiled=True)]
    while x72 -> x0, local copies, waits for them, and re-layouts: 11.9 us -> none
    unnamed x30 -> x51, local copies, waits for them, and re-layouts: 6.63 us -> 17.4 us
  transfers between devices with their start and end apart: 3 -> 5, of which waited for: 0 -> 2; matrix products, arithmetic and copies ran while one was open for 82% -> 2% of each run, Pallas kernels for 0% -> 24%
where the time goes in v1:
time: 106 us
  Pallas kernels  38.7 us (37%)
  waiting for transfers between devices  22.4 us (21%)
  local copies, waits for them, and re-layouts  19.1 us (18%)
  between operations  13.5 us (13%)
  starting transfers between devices  12.1 us (11%)
    pallas_call x1, Pallas kernels, near_field(): pl.pallas_call(near_kernel, out_shape=jax.ShapeDtypeStruct((OWN, RHS, LEA...  25.6 us
    all_gather x1, waiting for transfers between devices, on_device(): gathered = lax.all_gather(moments, AXES, axis=0, tiled=True)  19 us
    unnamed x51, local copies, waits for them, and re-layouts  17.4 us
    pallas_call x1, Pallas kernels, downward(): pl.pallas_call(downward_kernel, grid=(8,), out_shape=jax.ShapeDtypeStruct...  8.88 us
    ppermute x1, starting transfers between devices, on_device(): ch_before = lax.ppermute(charges[OWN - REACH:], AXES, up)  4.58 us
    pallas_call x1, Pallas kernels, upward(): pl.pallas_call(upward_kernel, grid=(8,), out_shape=jax.ShapeDtypeStruct((...  4.14 us
    ppermute x1, starting transfers between devices, on_device(): geo_before = lax.ppermute(geometry[OWN - REACH:], AXES, up)  3.63 us
    ppermute x1, waiting for transfers between devices, on_device(): geo_after = lax.ppermute(geometry[:REACH], AXES, down)  3.36 us
  transfers between devices with their start and end apart: 5, of which 2 were waited for; matrix products, arithmetic and copies ran while one was open for 2% of the time, Pallas kernels for 24%

profile of v1, /device:TPU:1, one launch (start us, length us, event | category | flops | bytes accessed | tf_op | source)
XLA Modules:
  0.0 105.8 jit_solution(11306636576772497018)
XLA Ops:
  6.5 1.6 %copy-done = f32[64,32,256]{2,1,0:T(8,128)S(1)} copy-done((f32[64,32,256]{2,1,0:T(8,128)S(1)}, f32[64,32,256]{2,1,0:T(8,128)}, u32[]{:S(2)}) %copy-start) | copy-done | bytes 2097176
  8.1 1.2 %copy-done.2 = f32[8,8,32,32]{3,2,1,0:T(8,128)S(1)} copy-done((f32[8,8,32,32]{3,2,1,0:T(8,128)S(1)}, f32[8,8,32,32]{3,2,1,0:T(8,128)}, u32[]{:S(2)}) %copy-start.2) | copy-done | bytes 262168
  9.4 1.2 %copy-done.4 = f32[64,16,256]{2,1,0:T(8,128)S(1)} copy-done((f32[64,16,256]{2,1,0:T(8,128)S(1)}, f32[64,16,256]{2,1,0:T(8,128)}, u32[]{:S(2)}) %copy-start.4) | copy-done | bytes 1048600
  10.6 0.9 copy-done.11
  11.5 4.1 %upward.1 = f32[1,16,384]{2,1,0:T(8,128)} custom-call(f32[64,16,256]{2,1,0:T(8,128)S(1)} %copy-done.4, f32[64,32,256]{2,1,0:T(8,128)S(1)} %copy-done, f32[8,8,32,32]{3,2,1,0:T(8,128)S(1)} %copy-done.2, f32[1,8,32,32]{3,2,1,0:T(8,128)S(1)} %copy-done.11), custom_call_target="tpu_custom_call" | custom-call | flops 100000000 | bytes 5000000 | tf_op jit(solution)/shard_map/upward/pallas_call | solution.py:71
  15.7 1.0 fusion
  16.7 4.6 %collective-permute-start.2 = (f32[32,16,256]{2,1,0:T(8,128)}, f32[32,16,256]{2,1,0:T(8,128)}, u32[]{:S(2)}, u32[]{:S(2)}) collective-permute-start(f32[32,16,256]{2,1,0:T(8,128)} %get-tuple-element.6), channel_id=1, source_target_pairs={{0,1},{1,2},{2,3},{3,4},{4,5},{5,6},{6,7},{7,8},{8,9},{9,10},{10,1... | collective-permute-start | bytes 1572872 | tf_op jit(solution)/shard_map/ppermute | solution.py:303
  21.3 1.9 %collective-permute-start.3 = (f32[32,16,256]{2,1,0:T(8,128)}, f32[32,16,256]{2,1,0:T(8,128)}, u32[]{:S(2)}, u32[]{:S(2)}) collective-permute-start(f32[32,16,256]{2,1,0:T(8,128)} %get-tuple-element.5), channel_id=1, source_target_pairs={{1,0},{2,1},{3,2},{4,3},{5,4},{6,5},{7,6},{8,7},{9,8},{10,9},{11,1... | collective-permute-start | bytes 1572872 | tf_op jit(solution)/shard_map/ppermute | solution.py:304
  23.9 3.6 %collective-permute-start = (f32[32,4,256]{2,1,0:T(4,128)}, f32[32,4,256]{2,1,0:T(4,128)S(1)}, u32[]{:S(2)}, u32[]{:S(2)}) collective-permute-start(f32[32,4,256]{2,1,0:T(4,128)} %get-tuple-element.8), channel_id=1, source_target_pairs={{0,1},{1,2},{2,3},{3,4},{4,5},{5,6},{6,7},{7,8},{8,9},{9,10},{10,1... | collective-permute-start | bytes 393224 | tf_op jit(solution)/shard_map/ppermute | solution.py:301
  27.5 1.9 %collective-permute-start.1 = (f32[32,4,256]{2,1,0:T(4,128)S(1)}, f32[32,4,256]{2,1,0:T(4,128)S(1)}, u32[]{:S(2)}, u32[]{:S(2)}) collective-permute-start(f32[32,4,256]{2,1,0:T(4,128)S(1)} %get-tuple-element.7), channel_id=1, source_target_pairs={{1,0},{2,1},{3,2},{4,3},{5,4},{6,5},{7,6},{8,7},{9,8},{10,9},{11,1... | collective-permute-start | bytes 393224 | tf_op jit(solution)/shard_map/ppermute | solution.py:302
  29.5 0.7 copy.13.near_list
  30.9 3.4 %collective-permute-done.1.geo_after = f32[32,4,256]{2,1,0:T(4,128)S(1)} collective-permute-done((f32[32,4,256]{2,1,0:T(4,128)S(1)}, f32[32,4,256]{2,1,0:T(4,128)S(1)}, u32[]{:S(2)}, u32[]{:S(2)}) %collective-permute-start.1) | collective-permute-done | bytes 131104 | tf_op jit(solution)/shard_map/ppermute | solution.py:302
  35.0 1.2 %copy-done.6 = f32[64,16,256]{2,1,0:T(8,128)S(1)} copy-done((f32[64,16,256]{2,1,0:T(8,128)S(1)}, f32[64,16,256]{2,1,0:T(8,128)}, u32[]{:S(2)}) %copy-start.6) | copy-done | bytes 1048600
  36.2 0.9 copy-done.15
  37.1 0.8 copy-done.16
  37.9 0.9 copy-done.20
  38.8 0.9 copy-done.22
  39.7 25.6 %near_field.1.near = f32[64,16,256]{2,1,0:T(8,128)S(1)} custom-call(s32[2]{0:T(128)S(1)} %pad_add_fusion.place, s32[64,12]{1,0:T(8,128)S(1)} %copy-done.16, s32[64]{0:T(128)S(1)} %copy-done.23, f32[64,4,256]{2,1,0:T(4,128)S(1)} %copy-done.15, f32[32,4,256]{2,1,0:T(4,128)S(1)} %copy-done.20, f32[32,4,256]{2,1,0:T(4,128)S(1)} %copy-done.22, ...), custom_call_target="tpu_custom_call" | custom-call | flops 20000000000 | bytes 4000000 | tf_op jit(solution)/shard_map/near_field/pallas_call | solution.py:210
  65.4 1.0 copy-done.9
  66.3 19.0 %all-gather.2.cloned.1.call-done.gathered = f32[128,16,384]{2,1,0:T(8,128)} async-done(((f32[1,16,384]{2,1,0:T(8,128)}), f32[128,16,384]{2,1,0:T(8,128)}) %all-gather.2.cloned.1.call-update) | async-done | bytes 3145744 | tf_op jit(solution)/shard_map/all_gather | solution.py:306
  85.4 1.9 %copy-done.7 = f32[128,16,384]{2,1,0:T(8,128)S(1)} copy-done((f32[128,16,384]{2,1,0:T(8,128)S(1)}, f32[128,16,384]{2,1,0:T(8,128)}, u32[]{:S(2)}) %copy-start.7) | copy-done | bytes 3145752
  87.3 1.6 %copy-done.8 = f32[8,16,32,32]{3,2,1,0:T(8,128)S(1)} copy-done((f32[8,16,32,32]{3,2,1,0:T(8,128)S(1)}, f32[8,16,32,32]{3,2,1,0:T(8,128)}, u32[]{:S(2)}) %copy-start.8) | copy-done | bytes 524312
  88.8 1.2 %copy-done.10 = f32[64,16,256]{2,1,0:T(8,128)S(1)} copy-done((f32[64,16,256]{2,1,0:T(8,128)S(1)}, f32[64,16,256]{2,1,0:T(8,128)}, u32[]{:S(2)}) %copy-start.10) | copy-done | bytes 1048600
  90.1 8.9 %downward.1 = f32[64,16,256]{2,1,0:T(8,128)} custom-call(s32[8,16]{1,0:T(8,128)S(1)} %copy-done.17, s32[1,16]{1,0:T(1,128)S(1)} %copy-done.18, f32[128,16,384]{2,1,0:T(8,128)S(1)} %copy-done.7, f32[1,16,32,32]{3,2,1,0:T(8,128)S(1)} %copy-done.13, f32[1,8,32,32]{3,2,1,0:T(8,128)S(1)} %copy-done.12, f32[8,16,32,32]{3,2,1,0:T(8,128)S(1)} %copy-done.8, ...), custom_call_target="tpu_custom_call" | custom-call | tf_op jit(solution)/shard_map/downward/pallas_call | solution.py:263
  (44 shorter events, 2.1 us)
Async XLA Ops:
  6.5 78.8 %all-gather.2.cloned.1.call-start = ((), (), s32[]{:S(2)}) async-start(), calls=%async_computation | async-start | bytes 3170304 | tf_op jit(solution)/shard_map/all_gather | solution.py:306
  6.5 1.6 %copy-start = (f32[64,32,256]{2,1,0:T(8,128)S(1)}, f32[64,32,256]{2,1,0:T(8,128)}, u32[]{:S(2)}) copy-start(f32[64,32,256]{2,1,0:T(8,128)} %basis.3) | copy-start | bytes 6291460
  8.1 1.2 %copy-start.2 = (f32[8,8,32,32]{3,2,1,0:T(8,128)S(1)}, f32[8,8,32,32]{3,2,1,0:T(8,128)}, u32[]{:S(2)}) copy-start(f32[8,8,32,32]{3,2,1,0:T(8,128)} %leaf_transfer.3) | copy-start | bytes 786436
  9.4 1.2 %copy-start.4 = (f32[64,16,256]{2,1,0:T(8,128)S(1)}, f32[64,16,256]{2,1,0:T(8,128)}, u32[]{:S(2)}) copy-start(f32[64,16,256]{2,1,0:T(8,128)} %charges.3) | copy-start | bytes 3145732
  11.5 4.2 %copy-start.5 = (f32[64,16,256]{2,1,0:T(8,128)S(1)}, f32[64,16,256]{2,1,0:T(8,128)}, u32[]{:S(2)}) copy-start(f32[64,16,256]{2,1,0:T(8,128)} %charges.3) | copy-start | bytes 3145732
  15.6 7.6 %copy-start.14 = (f32[64,4,256]{2,1,0:T(4,128)S(1)}, f32[64,4,256]{2,1,0:T(4,128)}, u32[]{:S(2)}) copy-start(f32[64,4,256]{2,1,0:T(4,128)} %geometry.1) | copy-start | bytes 786436
  15.6 13.8 %copy-start.24 = (s32[64,12]{0,1:T(8,128)S(1)}, s32[64,12]{0,1:T(8,128)}, u32[]{:S(2)}) copy-start(s32[64,12]{0,1:T(8,128)} %param.14) | copy-start | bytes 9220
  15.6 19.3 %copy-start.23 = (s32[64]{0:T(128)S(1)}, s32[64]{0:T(128)}, u32[]{:S(2)}) copy-start(s32[64]{0:T(128)} %near_count.1) | copy-start | bytes 772
  16.7 18.2 %collective-permute-start.2 = (f32[32,16,256]{2,1,0:T(8,128)}, f32[32,16,256]{2,1,0:T(8,128)}, u32[]{:S(2)}, u32[]{:S(2)}) collective-permute-start(f32[32,16,256]{2,1,0:T(8,128)} %get-tuple-element.6), channel_id=1, source_target_pairs={{0,1},{1,2},{2,3},{3,4},{4,5},{5,6},{6,7},{7,8},{8,9},{9,10},{10,1... | collective-permute-start | bytes 1572872 | tf_op jit(solution)/shard_map/ppermute | solution.py:303
  21.3 13.6 %collective-permute-start.3 = (f32[32,16,256]{2,1,0:T(8,128)}, f32[32,16,256]{2,1,0:T(8,128)}, u32[]{:S(2)}, u32[]{:S(2)}) collective-permute-start(f32[32,16,256]{2,1,0:T(8,128)} %get-tuple-element.5), channel_id=1, source_target_pairs={{1,0},{2,1},{3,2},{4,3},{5,4},{6,5},{7,6},{8,7},{9,8},{10,9},{11,1... | collective-permute-start | bytes 1572872 | tf_op jit(solution)/shard_map/ppermute | solution.py:304
  23.9 6.4 %collective-permute-start = (f32[32,4,256]{2,1,0:T(4,128)}, f32[32,4,256]{2,1,0:T(4,128)S(1)}, u32[]{:S(2)}, u32[]{:S(2)}) collective-permute-start(f32[32,4,256]{2,1,0:T(4,128)} %get-tuple-element.8), channel_id=1, source_target_pairs={{0,1},{1,2},{2,3},{3,4},{4,5},{5,6},{6,7},{7,8},{8,9},{9,10},{10,1... | collective-permute-start | bytes 393224 | tf_op jit(solution)/shard_map/ppermute | solution.py:301
  27.5 6.7 %collective-permute-start.1 = (f32[32,4,256]{2,1,0:T(4,128)S(1)}, f32[32,4,256]{2,1,0:T(4,128)S(1)}, u32[]{:S(2)}, u32[]{:S(2)}) collective-permute-start(f32[32,4,256]{2,1,0:T(4,128)S(1)} %get-tuple-element.7), channel_id=1, source_target_pairs={{1,0},{2,1},{3,2},{4,3},{5,4},{6,5},{7,6},{8,7},{9,8},{10,9},{11,1... | collective-permute-start | bytes 393224 | tf_op jit(solution)/shard_map/ppermute | solution.py:302
  30.2 55.1 %copy-start.17 = (s32[8,16]{1,0:T(8,128)S(1)}, s32[8,16]{1,0:T(8,128)}, u32[]{:S(2)}) copy-start(s32[8,16]{1,0:T(8,128)} %box_far_list.1) | copy-start | bytes 1540
  30.2 55.1 %copy-start.18 = (s32[1,16]{1,0:T(1,128)S(1)}, s32[1,16]{1,0:T(1,128)}, u32[]{:S(2)}) copy-start(s32[1,16]{1,0:T(1,128)} %top_far_list.1) | copy-start | bytes 196
  30.3 55.1 %copy-start.1 = (f32[64,32,256]{2,1,0:T(8,128)S(1)}, f32[64,32,256]{2,1,0:T(8,128)}, u32[]{:S(2)}) copy-start(f32[64,32,256]{2,1,0:T(8,128)} %basis.3) | copy-start | bytes 6291460
  30.3 55.1 %copy-start.3 = (f32[8,8,32,32]{3,2,1,0:T(8,128)S(1)}, f32[8,8,32,32]{3,2,1,0:T(8,128)}, u32[]{:S(2)}) copy-start(f32[8,8,32,32]{3,2,1,0:T(8,128)} %leaf_transfer.3) | copy-start | bytes 786436
  34.9 1.2 %copy-start.6 = (f32[64,16,256]{2,1,0:T(8,128)S(1)}, f32[64,16,256]{2,1,0:T(8,128)}, u32[]{:S(2)}) copy-start(f32[64,16,256]{2,1,0:T(8,128)} %charges.3) | copy-start | bytes 3145732
  36.2 0.9 copy-start.15
  39.7 45.7 %copy-start.12 = (f32[1,8,32,32]{3,2,1,0:T(8,128)S(1)}, f32[1,8,32,32]{3,2,1,0:T(8,128)}, u32[]{:S(2)}) copy-start(f32[1,8,32,32]{3,2,1,0:T(8,128)} %box_transfer.3) | copy-start | bytes 98308
  39.7 45.7 %copy-start.13 = (f32[1,16,32,32]{3,2,1,0:T(8,128)S(1)}, f32[1,16,32,32]{3,2,1,0:T(8,128)}, u32[]{:S(2)}) copy-start(f32[1,16,32,32]{3,2,1,0:T(8,128)} %top_coupling.1) | copy-start | bytes 196612
  65.4 1.0 copy-start.9
  85.4 1.9 %copy-start.7 = (f32[128,16,384]{2,1,0:T(8,128)S(1)}, f32[128,16,384]{2,1,0:T(8,128)}, u32[]{:S(2)}) copy-start(f32[128,16,384]{2,1,0:T(8,128)} %all-gather.2.cloned.1.call-done.gathered) | copy-start | bytes 9437188
  87.3 1.6 %copy-start.8 = (f32[8,16,32,32]{3,2,1,0:T(8,128)S(1)}, f32[8,16,32,32]{3,2,1,0:T(8,128)}, u32[]{:S(2)}) copy-start(f32[8,16,32,32]{3,2,1,0:T(8,128)} %box_coupling.1) | copy-start | bytes 1572868
  88.8 1.2 %copy-start.10 = (f32[64,16,256]{2,1,0:T(8,128)S(1)}, f32[64,16,256]{2,1,0:T(8,128)}, u32[]{:S(2)}) copy-start(f32[64,16,256]{2,1,0:T(8,128)} %copy-done.9) | copy-start | bytes 3145732
  (6 other events, 4.8 us)
Sparse Core Ops, SparseCore 0:
  15.8 69.5 all-gather.1

commit v2 on v1

--- a/solution.py
+++ b/solution.py
@@ -21,6 +21,7 @@
 OWN = 64
 WIDE = OWN + 2 * REACH
 UNROLL = 12
+VMEM = 60 * 2**20
 FEATURES = 48
 EXTENT = 8.0
 
@@ -53,48 +54,142 @@
     return both[:rows] + both[rows:] + dot(ah, bl, dims)
 
 
-def upward_kernel(charges, basis, leaf_transfer, box_transfer, out, moments):
-    box = pl.program_id(0)
-    parts = [dot3(charges[c], basis[c], NT) for c in range(8)]
-    leaf_moments = jnp.concatenate(parts, axis=1)
-    moments[box] = dot3(leaf_moments, leaf_transfer[...].reshape(8 * RANK, RANK), NN)
-
-    @pl.when(box == 7)
-    def _():
-        boxes = jnp.concatenate([moments[b] for b in range(8)], axis=1)
-        top = dot3(boxes, box_transfer[...].reshape(8 * RANK, RANK), NN)
-        out[0, :, : 8 * RANK] = boxes
-        out[0, :, 8 * RANK :] = jnp.concatenate([top, jnp.zeros((RHS, 128 - RANK), f32)], axis=1)
-
-
-def upward(charges, basis, leaf_transfer, box_transfer):
+ORDERS = ((0, 1, 2), (1, 2, 0), (2, 0, 1))
+
+
+def coordinates(device):
+    return (device // 32, (device // 2) % 4, (device // 8) % 4), device % 2
+
+
+def row_in(part, chip, core):
+    first, second, third = (chip[axis] for axis in ORDERS[part])
+    return ((core * 4 + third) * 4 + second) * 4 + first
+
+
+def exchange_kernel(
+    geometry, charges_far, charges, basis, leaf_transfer, box_transfer,
+    gathered, geo_halo, ch_halo, moments, send, receive, halo_send, halo_receive,
+):
+    me = lax.axis_index("group") * 32 + lax.axis_index("dev")
+    chip, core = coordinates(me)
+
+    def device(chip, core):
+        return (chip[0], (chip[2] * 4 + chip[1]) * 2 + core)
+
+    def peer(axis, step):
+        moved = list(chip)
+        moved[axis] = (chip[axis] + step) % 4
+        return device(moved, core)
+
+    sibling = device(chip, 1 - core)
+    above = (me + 1) % 128
+    below = (me + 127) % 128
+    above = (above // 32, above % 32)
+    below = (below // 32, below % 32)
+
+    barrier = pltpu.get_barrier_semaphore()
+    partners = [peer(axis, step) for axis in range(3) for step in (1, 2, 3)] + [sibling, above, below]
+    for partner in partners:
+        pl.semaphore_signal(barrier, inc=1, device_id=partner, device_id_type=pl.DeviceIdType.MESH)
+
+    def remote(source, target, sent, received, partner):
+        return pltpu.make_async_remote_copy(
+            src_ref=source, dst_ref=target, send_sem=sent, recv_sem=received,
+            device_id=partner, device_id_type=pl.DeviceIdType.MESH,
+        )
+
+    def box_moments(box, carry):
+        parts = [dot3(charges[box * 8 + c], basis[box * 8 + c], NT) for c in range(8)]
+        transfer = leaf_transfer[box].reshape(8 * RANK, RANK)
+        moments[box] = dot3(jnp.concatenate(parts, axis=1), transfer, NN)
+        return carry
+
+    box_moments(0, 0)
+    pl.semaphore_wait(barrier, len(partners))
+    halo = [
+        remote(geometry.at[pl.ds(OWN - REACH, REACH)], geo_halo.at[0], halo_send.at[0], halo_receive.at[0], above),
+        remote(geometry.at[pl.ds(0, REACH)], geo_halo.at[1], halo_send.at[1], halo_receive.at[1], below),
+        remote(charges_far.at[pl.ds(OWN - REACH, REACH)], ch_halo.at[0], halo_send.at[2], halo_receive.at[2], above),
+        remote(charges_far.at[pl.ds(0, REACH)], ch_halo.at[1], halo_send.at[3], halo_receive.at[3], below),
+    ]
+    for copy in halo:
+        copy.start()
+    lax.fori_loop(1, 8, box_moments, 0)
+    boxes = jnp.concatenate([moments[b] for b in range(8)], axis=1)
+    top = dot3(boxes, box_transfer[...].reshape(8 * RANK, RANK), NN)
+    own = [row_in(part, chip, core) for part in range(3)]
+    gathered[0, own[0]] = boxes[:, :128]
+    gathered[1, own[1]] = boxes[:, 128:]
+    gathered[2, own[2]] = jnp.concatenate([top, jnp.zeros((RHS, 128 - RANK), f32)], axis=1)
+
+    everything = list(halo)
+    waiting = []
+    for stage in range(3):
+        size = 4**stage
+        running = []
+        for part in range(3):
+            axis = ORDERS[part][stage]
+            first = (own[part] // size) * size
+            block = gathered.at[part, pl.ds(first, size)]
+            for step in (1, 2, 3):
+                slot = 3 * stage + step - 1
+                copy = remote(block, block, send.at[part, slot], receive.at[part, slot], peer(axis, step))
+                copy.start()
+                running.append((part, step, copy))
+            if stage == 2:
+                copy = remote(block, block, send.at[part, 9], receive.at[part, 9], sibling)
+                copy.start()
+                waiting.append(copy)
+        for part, step, copy in running:
+            copy.wait_recv()
+            if stage == 2:
+                axis = ORDERS[part][2]
+                third = (chip[axis] + 4 - step) % 4
+                block = gathered.at[part, pl.ds((core * 4 + third) * 16, 16)]
+                forward = remote(block, block, send.at[part, 9 + step], receive.at[part, 9 + step], sibling)
+                forward.start()
+                waiting.append(forward)
+            everything.append(copy)
+    for copy in waiting:
+        copy.wait_recv()
+    for copy in halo:
+        copy.wait_recv()
+    for copy in everything + waiting:
+        copy.wait_send()
+
+
+def exchange(geometry, charges, basis, leaf_transfer, box_transfer):
+    far = pl.BlockSpec(memory_space=pl.ANY)
+    vmem = pl.BlockSpec(memory_space=pltpu.VMEM)
     return pl.pallas_call(
-        upward_kernel,
-        grid=(8,),
-        out_shape=jax.ShapeDtypeStruct((1, RHS, 8 * RANK + 128), f32),
-        in_specs=[
-            pl.BlockSpec((8, RHS, LEAF), lambda b: (b, 0, 0)),
-            pl.BlockSpec((8, RANK, LEAF), lambda b: (b, 0, 0)),
-            pl.BlockSpec((1, 8, RANK, RANK), lambda b: (b, 0, 0, 0)),
-            pl.BlockSpec((1, 8, RANK, RANK), lambda b: (0, 0, 0, 0)),
+        exchange_kernel,
+        out_shape=(
+            jax.ShapeDtypeStruct((3, 128, RHS, 128), f32),
+            jax.ShapeDtypeStruct((2, REACH, 4, LEAF), f32),
+            jax.ShapeDtypeStruct((2, REACH, RHS, LEAF), f32),
+        ),
+        in_specs=[far, far, vmem, vmem, vmem, vmem],
+        out_specs=(vmem, far, far),
+        scratch_shapes=[
+            pltpu.VMEM((8, RHS, RANK), f32),
+            pltpu.SemaphoreType.DMA((3, 13)),
+            pltpu.SemaphoreType.DMA((3, 13)),
+            pltpu.SemaphoreType.DMA((4,)),
+            pltpu.SemaphoreType.DMA((4,)),
         ],
-        out_specs=pl.BlockSpec((1, RHS, 8 * RANK + 128), lambda b: (0, 0, 0)),
-        scratch_shapes=[pltpu.VMEM((8, RHS, RANK), f32)],
-        compiler_params=pltpu.CompilerParams(vmem_limit_bytes=16 * 2**20),
-        cost_estimate=pl.CostEstimate(flops=10**8, bytes_accessed=5 * 10**6, transcendentals=0),
-        name="upward",
-    )(charges, basis, leaf_transfer, box_transfer)
+        compiler_params=pltpu.CompilerParams(vmem_limit_bytes=VMEM, collective_id=0, has_side_effects=True),
+        name="exchange",
+    )(geometry, charges, charges, basis, leaf_transfer, box_transfer)
 
 
 def near_kernel(
-    place, near_list, near_count, geometry, geo_before, geo_after, charges, ch_before, ch_after,
+    near_list, near_count, geometry, geo_halo, charges, ch_halo,
     out, geo, source, source_rows, target_rows, block_hi, block_lo, total, extent,
 ):
-    me = place[0]
-    offset = me * OWN - REACH
-    geo[0:REACH] = geo_before[...]
+    offset = lax.axis_index(AXES) * OWN - REACH
+    geo[0:REACH] = geo_halo[0]
     geo[REACH : REACH + OWN] = geometry[...]
-    geo[REACH + OWN :] = geo_after[...]
+    geo[REACH + OWN :] = geo_halo[1]
     centre = jnp.broadcast_to(jnp.mean(geometry[OWN // 2], axis=1, keepdims=True), (4, LEAF))
     one = jnp.ones((1, LEAF), f32)
     rest = jnp.zeros((3, LEAF), f32)
@@ -111,9 +206,9 @@
 
         lax.fori_loop(0, part.shape[0], leaf, 0, unroll=8)
 
-    weigh(ch_before, 0)
+    weigh(ch_halo.at[0], 0)
     weigh(charges, REACH)
-    weigh(ch_after, REACH + OWN)
+    weigh(ch_halo.at[1], REACH + OWN)
 
     def target(n, largest):
         v = geo[n + REACH] - centre
@@ -129,7 +224,7 @@
         a, b, c = thirds(jnp.concatenate([-2.0 * v[0:3], norm, one, rest], axis=0))
         source_rows[n, :, :FEATURES] = jnp.concatenate([a, b, a, b, c, a], axis=0).astype(bf16).T
         leaf = offset + n
-        held = (leaf >= 0) & (leaf < place[1])
+        held = (leaf >= 0) & (leaf < lax.axis_size(AXES) * OWN)
         return jnp.maximum(largest, jnp.where(held, norm, 0.0))
 
     nothing = jnp.zeros((1, LEAF), f32)
@@ -204,13 +299,13 @@
     out[...] = total[0:OWN]
 
 
-def near_field(place, near_list, near_count, *arrays):
+def near_field(near_list, near_count, *arrays):
     smem = pl.BlockSpec(memory_space=pltpu.SMEM)
     vmem = pl.BlockSpec(memory_space=pltpu.VMEM)
     return pl.pallas_call(
         near_kernel,
         out_shape=jax.ShapeDtypeStruct((OWN, RHS, LEAF), f32),
-        in_specs=[smem] * 3 + [vmem] * 6,
+        in_specs=[smem] * 2 + [vmem] * 4,
         out_specs=vmem,
         scratch_shapes=[
             pltpu.VMEM((WIDE, 4, LEAF), f32),
@@ -222,10 +317,10 @@
             pltpu.VMEM((OWN + 1, RHS, LEAF), f32),
             pltpu.SMEM((1,), f32),
         ],
-        compiler_params=pltpu.CompilerParams(vmem_limit_bytes=40 * 2**20),
+        compiler_params=pltpu.CompilerParams(vmem_limit_bytes=VMEM),
         cost_estimate=pl.CostEstimate(flops=2 * 10**10, bytes_accessed=4 * 10**6, transcendentals=5 * 10**7),
         name="near_field",
-    )(place, near_list, near_count, *arrays)
+    )(near_list, near_count, *arrays)
 
 
 def downward_kernel(
@@ -238,7 +333,8 @@
     def _():
         top_local = jnp.zeros((RHS, RANK), f32)
         for f in range(FAR):
-            top = gathered[top_far_list[0, f], :, 8 * RANK : 8 * RANK + RANK]
+            chip, core = coordinates(top_far_list[0, f])
+            top = gathered[2, row_in(2, chip, core), :, :RANK]
             top_local = top_local + dot3(top, top_coupling[0, f], NN)
         down = dot3(top_local, box_transfer[...].reshape(8 * RANK, RANK), NT)
         for b in range(8):
@@ -247,10 +343,10 @@
     local = box_down[box]
     for f in range(FAR):
         far = box_far_list[box, f]
-        lane = (far % 8) * RANK
-        base = pl.multiple_of((lane // 128) * 128, 128)
-        tile = gathered[far // 8, :, pl.ds(base, 128)]
-        tile = pltpu.roll(tile, (128 - lane % 128) % 128, 1)
+        chip, core = coordinates(far // 8)
+        part = (far % 8) // 4
+        row = jnp.where(part == 0, row_in(0, chip, core), row_in(1, chip, core))
+        tile = pltpu.roll(gathered[part, row], (4 - far % 4) % 4 * RANK, 1)
         local = local + dot3(tile[:, :RANK], box_coupling[0, f], NN)
     leaves = dot3(local, leaf_transfer[...].reshape(8 * RANK, RANK), NT)
     for c in range(8):
@@ -277,7 +373,7 @@
         ],
         out_specs=pl.BlockSpec((8, RHS, LEAF), lambda b: (b, 0, 0)),
         scratch_shapes=[pltpu.VMEM((8, RHS, RANK), f32)],
-        compiler_params=pltpu.CompilerParams(vmem_limit_bytes=24 * 2**20),
+        compiler_params=pltpu.CompilerParams(vmem_limit_bytes=VMEM),
         name="downward",
     )(box_far_list, top_far_list, gathered, top_coupling, box_transfer, box_coupling, leaf_transfer, basis, near)
 
@@ -295,19 +391,8 @@
     top_far_list,
     top_coupling,
 ):
-    size = lax.axis_size(AXES)
-    up = [(i, i + 1) for i in range(size - 1)]
-    down = [(i + 1, i) for i in range(size - 1)]
-    geo_before = lax.ppermute(geometry[OWN - REACH :], AXES, up)
-    geo_after = lax.ppermute(geometry[:REACH], AXES, down)
-    ch_before = lax.ppermute(charges[OWN - REACH :], AXES, up)
-    ch_after = lax.ppermute(charges[:REACH], AXES, down)
-    moments = upward(charges, leaf_cluster_basis, leaf_transfer, box_transfer)
-    gathered = lax.all_gather(moments, AXES, axis=0, tiled=True)
-    place = jnp.stack([lax.axis_index(AXES), jnp.int32(size * OWN)]).astype(jnp.int32)
-    near = near_field(
-        place, near_list, near_count, geometry, geo_before, geo_after, charges, ch_before, ch_after
-    )
+    gathered, geo_halo, ch_halo = exchange(geometry, charges, leaf_cluster_basis, leaf_transfer, box_transfer)
+    near = near_field(near_list, near_count, geometry, geo_halo, charges, ch_halo)
     return downward(
         box_far_list, top_far_list, gathered, top_coupling, box_transfer, box_coupling, leaf_transfer,
         leaf_cluster_basis, near,

time: 106 us -> 91.9 us (0.87)
  Pallas kernels: 38.7 us -> 90.2 us
  waiting for transfers between devices: 22.4 us -> 0 us
  local copies, waits for them, and re-layouts: 19.1 us -> 1.4 us
  between operations: 13.5 us -> 0.01 us
  starting transfers between devices: 12.1 us -> 0 us
    pallas_call x1, Pallas kernels: 4.14 us -> 38.4 us  [exchange(): pl.pallas_call(exchange_kernel, out_shape=(jax.ShapeDtypeStruct((3, 128,...]
    all_gather x1 -> x0, waiting for transfers between devices: 19 us -> none  [on_device(): gathered = lax.all_gather(moments, AXES, axis=0, tiled=True)]
    unnamed x51 -> x1, local copies, waits for them, and re-layouts: 17.4 us -> 1.4 us
    pallas_call x1, Pallas kernels: 25.6 us -> 38.4 us  [near_field(): pl.pallas_call(near_kernel, out_shape=jax.ShapeDtypeStruct((OWN, RHS, LEA...]
    ppermute x4 -> x0, starting transfers between devices: 12.1 us -> none  [the longest x1 4.58 us: on_device(): ch_before = lax.ppermute(charges[OWN - REACH:], AXES, up)]
    pallas_call x1, Pallas kernels: 8.88 us -> 13.3 us  [downward(): pl.pallas_call(downward_kernel, grid=(8,), out_shape=jax.ShapeDtypeStruct...]
    ppermute x4 -> x0, waiting for transfers between devices: 3.37 us -> none  [the longest x1 3.36 us: on_device(): geo_after = lax.ppermute(geometry[:REACH], AXES, down)]
    slice x2 -> x0, local copies, waits for them, and re-layouts: 1.71 us -> none  [the longest x1 1.05 us: on_device(): ch_after = lax.ppermute(charges[:REACH], AXES, down)]
  transfers between devices with their start and end apart: 5 -> 0, of which waited for: 2 -> 0; matrix products, arithmetic and copies ran while one was open for 2% -> 0% of each run, Pallas kernels for 24% -> 0%
where the time goes in v2:
time: 91.9 us; the launch traced here: 91.6 us
  Pallas kernels  90.2 us (98%)
  local copies, waits for them, and re-layouts  1.4 us (2%)
    pallas_call x1, Pallas kernels, near_field(): pl.pallas_call(near_kernel, out_shape=jax.ShapeDtypeStruct((OWN, RHS, LEA...  38.4 us
    pallas_call x1, Pallas kernels, exchange(): pl.pallas_call(exchange_kernel, out_shape=(jax.ShapeDtypeStruct((3, 128,...  38.4 us
    pallas_call x1, Pallas kernels, downward(): pl.pallas_call(downward_kernel, grid=(8,), out_shape=jax.ShapeDtypeStruct...  13.3 us

profile of v2, /device:TPU:1, one launch (start us, length us, event | category | flops | bytes accessed | tf_op | source)
XLA Modules:
  0.0 91.6 jit_solution(3296118055295465880)
XLA Ops:
  0.0 1.4 %copy.12.near_list = s32[64,12]{1,0:T(8,128)} copy(s32[64,12]{0,1:T(8,128)} %param.14) | data formatting | bytes 6144 | tf_op args[3]
  1.4 38.4 %exchange.1 = (f32[3,128,16,128]{3,2,1,0:T(8,128)}, f32[2,32,4,256]{3,2,1,0:T(4,128)}, f32[2,32,16,256]{3,2,1,0:T(8,128)}) custom-call(f32[64,4,256]{2,1,0:T(4,128)} %geometry.3, f32[64,16,256]{2,1,0:T(8,128)} %charges.3, f32[64,16,256]{2,1,0:T(8,128)} %charges.3, f32[64,32,256]{2,1,0:T(8,128)} %basis.3, f32[8,8,32,32]{3,2,1,0:T(8,128)} %leaf_transfer.3, ...), custom_call_target="tpu_custom_call" | custom-call | tf_op jit(solution)/shard_map/exchange/pallas_call | solution.py:164
  39.8 38.4 %near_field.1.near = f32[64,16,256]{2,1,0:T(8,128)} custom-call(s32[64,12]{1,0:T(8,128)} %copy.12.near_list, s32[64]{0:T(128)} %near_count.1, f32[64,4,256]{2,1,0:T(4,128)} %geometry.3, f32[2,32,4,256]{3,2,1,0:T(4,128)} %get-tuple-element.9.geo_halo, f32[64,16,256]{2,1,0:T(8,128)} %charges.3, f32[2,32,16,256]{3,2,1,0:T(8,128)} %get-tuple-element.10.ch_halo), custom_call_target="tpu_custom_call" | custom-call | flops 20000000000 | bytes 4000000 | tf_op jit(solution)/shard_map/near_field/pallas_call | solution.py:305
  78.3 13.3 %downward.1 = f32[64,16,256]{2,1,0:T(8,128)} custom-call(s32[8,16]{1,0:T(8,128)} %box_far_list.1, s32[1,16]{1,0:T(1,128)} %top_far_list.1, f32[3,128,16,128]{3,2,1,0:T(8,128)} %get-tuple-element.8.gathered, f32[1,16,32,32]{3,2,1,0:T(8,128)} %top_coupling.1, f32[1,8,32,32]{3,2,1,0:T(8,128)} %box_transfer.3, f32[8,16,32,32]{3,2,1,0:T(8,128)} %box_coupling.1, ...), custom_call_target="tpu_custom_call" | custom-call | tf_op jit(solution)/shard_map/downward/pallas_call | solution.py:359

commit v3 on v2

--- a/solution.py
+++ b/solution.py
@@ -20,7 +20,7 @@
 REACH = 32
 OWN = 64
 WIDE = OWN + 2 * REACH
-UNROLL = 12
+UNROLL = 16
 VMEM = 60 * 2**20
 FEATURES = 48
 EXTENT = 8.0
@@ -58,12 +58,12 @@
 
 
 def coordinates(device):
-    return (device // 32, (device // 2) % 4, (device // 8) % 4), device % 2
+    return (device >> 5, (device >> 1) & 3, (device >> 3) & 3), device & 1
 
 
 def row_in(part, chip, core):
     first, second, third = (chip[axis] for axis in ORDERS[part])
-    return ((core * 4 + third) * 4 + second) * 4 + first
+    return (core << 6) + (third << 4) + (second << 2) + first
 
 
 def exchange_kernel(
@@ -182,10 +182,21 @@
     )(geometry, charges, charges, basis, leaf_transfer, box_transfer)
 
 
-def near_kernel(
-    near_list, near_count, geometry, geo_halo, charges, ch_halo,
+def local_kernel(
+    near_list, near_count, box_far_list, top_far_list, geometry, geo_halo, charges, ch_halo,
+    gathered_far, top_coupling_far, box_transfer_far, box_coupling_far, leaf_transfer_far, basis_far,
     out, geo, source, source_rows, target_rows, block_hi, block_lo, total, extent,
+    gathered, top_coupling, box_transfer, box_coupling, leaf_transfer, basis, arrived,
 ):
+    loads = [
+        pltpu.make_async_copy(far, here, arrived.at[n])
+        for n, (far, here) in enumerate((
+            (gathered_far, gathered), (top_coupling_far, top_coupling), (box_transfer_far, box_transfer),
+            (box_coupling_far, box_coupling), (leaf_transfer_far, leaf_transfer), (basis_far, basis),
+        ))
+    ]
+    for load in loads:
+        load.start()
     offset = lax.axis_index(AXES) * OWN - REACH
     geo[0:REACH] = geo_halo[0]
     geo[REACH : REACH + OWN] = geometry[...]
@@ -296,16 +307,61 @@
 
         lax.fori_loop(0, OWN, leaf_sum, 0)
 
-    out[...] = total[0:OWN]
-
-
-def near_field(near_list, near_count, *arrays):
+    for load in loads:
+        load.wait()
+    downward(
+        box_far_list, top_far_list, gathered, top_coupling, box_transfer, box_coupling, leaf_transfer, basis, total, out
+    )
+
+
+def picked(rows, lane):
+    tiles = []
+    for g in range(0, FAR, 4):
+        tile = rows[g + 3]
+        for k in (2, 1, 0):
+            tile = jnp.where(lane < (k + 1) * RANK, rows[g + k], tile)
+        tiles.append(tile)
+    return jnp.concatenate(tiles, axis=1)
+
+
+def downward(
+    box_far_list, top_far_list, gathered, top_coupling, box_transfer, box_coupling, leaf_transfer, basis, total, out
+):
+    lane = lax.broadcasted_iota(jnp.int32, (RHS, 128), 1)
+    rows = []
+    for f in range(FAR):
+        chip, core = coordinates(top_far_list[0, f])
+        tile = gathered[2, row_in(2, chip, core)]
+        rows.append(pltpu.roll(tile, f % 4 * RANK, 1) if f % 4 else tile)
+    top_local = dot3(picked(rows, lane), top_coupling[0].reshape(FAR * RANK, RANK), NN)
+    down = dot3(top_local, box_transfer[0].reshape(8 * RANK, RANK), NT)
+    for box in range(8):
+        rows = []
+        for f in range(FAR):
+            far = box_far_list[box, f]
+            chip, core = coordinates(far >> 3)
+            part = (far >> 2) & 1
+            row = jnp.where(part == 0, row_in(0, chip, core), row_in(1, chip, core))
+            rows.append(pltpu.roll(gathered[part, row], ((f - far) & 3) * RANK, 1))
+        local = dot3(picked(rows, lane), box_coupling[box].reshape(FAR * RANK, RANK), NN)
+        local = local + down[:, box * RANK : (box + 1) * RANK]
+        leaves = dot3(local, leaf_transfer[box].reshape(8 * RANK, RANK), NT)
+        for c in range(8):
+            hi, lo = halves(leaves[:, c * RANK : (c + 1) * RANK])
+            base, rest = halves(basis[8 * box + c])
+            out[8 * box + c] = total[8 * box + c] + dot(
+                jnp.concatenate([hi, lo, hi], axis=1), jnp.concatenate([base, base, rest], axis=0), NN
+            )
+
+
+def local_part(*arrays):
     smem = pl.BlockSpec(memory_space=pltpu.SMEM)
     vmem = pl.BlockSpec(memory_space=pltpu.VMEM)
+    far = pl.BlockSpec(memory_space=pl.ANY)
     return pl.pallas_call(
-        near_kernel,
+        local_kernel,
         out_shape=jax.ShapeDtypeStruct((OWN, RHS, LEAF), f32),
-        in_specs=[smem] * 2 + [vmem] * 4,
+        in_specs=[smem] * 4 + [vmem] * 4 + [far] * 6,
         out_specs=vmem,
         scratch_shapes=[
             pltpu.VMEM((WIDE, 4, LEAF), f32),
@@ -316,66 +372,12 @@
             pltpu.VMEM((UNROLL, LEAF, LEAF), bf16),
             pltpu.VMEM((OWN + 1, RHS, LEAF), f32),
             pltpu.SMEM((1,), f32),
-        ],
+        ]
+        + [pltpu.VMEM(array.shape, f32) for array in arrays[8:]]
+        + [pltpu.SemaphoreType.DMA((6,))],
         compiler_params=pltpu.CompilerParams(vmem_limit_bytes=VMEM),
-        cost_estimate=pl.CostEstimate(flops=2 * 10**10, bytes_accessed=4 * 10**6, transcendentals=5 * 10**7),
-        name="near_field",
-    )(near_list, near_count, *arrays)
-
-
-def downward_kernel(
-    box_far_list, top_far_list, gathered, top_coupling, box_transfer, box_coupling, leaf_transfer, basis, near,
-    out, box_down,
-):
-    box = pl.program_id(0)
-
-    @pl.when(box == 0)
-    def _():
-        top_local = jnp.zeros((RHS, RANK), f32)
-        for f in range(FAR):
-            chip, core = coordinates(top_far_list[0, f])
-            top = gathered[2, row_in(2, chip, core), :, :RANK]
-            top_local = top_local + dot3(top, top_coupling[0, f], NN)
-        down = dot3(top_local, box_transfer[...].reshape(8 * RANK, RANK), NT)
-        for b in range(8):
-            box_down[b] = down[:, b * RANK : (b + 1) * RANK]
-
-    local = box_down[box]
-    for f in range(FAR):
-        far = box_far_list[box, f]
-        chip, core = coordinates(far // 8)
-        part = (far % 8) // 4
-        row = jnp.where(part == 0, row_in(0, chip, core), row_in(1, chip, core))
-        tile = pltpu.roll(gathered[part, row], (4 - far % 4) % 4 * RANK, 1)
-        local = local + dot3(tile[:, :RANK], box_coupling[0, f], NN)
-    leaves = dot3(local, leaf_transfer[...].reshape(8 * RANK, RANK), NT)
-    for c in range(8):
-        out[c] = near[c] + dot3(leaves[:, c * RANK : (c + 1) * RANK], basis[c], NN)
-
-
-def downward(box_far_list, top_far_list, gathered, top_coupling, box_transfer, box_coupling, leaf_transfer, basis, near):
-    smem = pl.BlockSpec(memory_space=pltpu.SMEM)
-    vmem = pl.BlockSpec(memory_space=pltpu.VMEM)
-    return pl.pallas_call(
-        downward_kernel,
-        grid=(8,),
-        out_shape=jax.ShapeDtypeStruct((OWN, RHS, LEAF), f32),
-        in_specs=[
-            smem,
-            smem,
-            vmem,
-            vmem,
-            vmem,
-            pl.BlockSpec((1, FAR, RANK, RANK), lambda b: (b, 0, 0, 0)),
-            pl.BlockSpec((1, 8, RANK, RANK), lambda b: (b, 0, 0, 0)),
-            pl.BlockSpec((8, RANK, LEAF), lambda b: (b, 0, 0)),
-            pl.BlockSpec((8, RHS, LEAF), lambda b: (b, 0, 0)),
-        ],
-        out_specs=pl.BlockSpec((8, RHS, LEAF), lambda b: (b, 0, 0)),
-        scratch_shapes=[pltpu.VMEM((8, RHS, RANK), f32)],
-        compiler_params=pltpu.CompilerParams(vmem_limit_bytes=VMEM),
-        name="downward",
-    )(box_far_list, top_far_list, gathered, top_coupling, box_transfer, box_coupling, leaf_transfer, basis, near)
+        name="local_part",
+    )(*arrays)
 
 
 def on_device(
@@ -392,10 +394,9 @@
     top_coupling,
 ):
     gathered, geo_halo, ch_halo = exchange(geometry, charges, leaf_cluster_basis, leaf_transfer, box_transfer)
-    near = near_field(near_list, near_count, geometry, geo_halo, charges, ch_halo)
-    return downward(
-        box_far_list, top_far_list, gathered, top_coupling, box_transfer, box_coupling, leaf_transfer,
-        leaf_cluster_basis, near,
+    return local_part(
+        near_list, near_count, box_far_list, top_far_list, geometry, geo_halo, charges, ch_halo,
+        gathered, top_coupling, box_transfer, box_coupling, leaf_transfer, leaf_cluster_basis,
     )
 
 

time: 91.9 us -> 79.3 us (0.86)
  Pallas kernels: 90.2 us -> 76.8 us
    pallas_call x2 -> x1, Pallas kernels: 51.8 us -> 38.3 us  [local_part(): pl.pallas_call(local_kernel, out_shape=jax.ShapeDtypeStruct((OWN, RHS, LE...]
where the time goes in v3:
time: 79.3 us; the launch traced here: 78.2 us
  Pallas kernels  76.8 us (97%)
  local copies, waits for them, and re-layouts  1.39 us (2%)
    pallas_call x1, Pallas kernels, exchange(): pl.pallas_call(exchange_kernel, out_shape=(jax.ShapeDtypeStruct((3, 128,...  38.4 us
    pallas_call x1, Pallas kernels, local_part(): pl.pallas_call(local_kernel, out_shape=jax.ShapeDtypeStruct((OWN, RHS, LE...  38.3 us

profile of v3, /device:TPU:1, one launch (start us, length us, event | category | flops | bytes accessed | tf_op | source)
XLA Modules:
  0.0 78.2 jit_solution(12418957802669233296)
XLA Ops:
  0.0 1.4 %copy.12.near_list = s32[64,12]{1,0:T(8,128)} copy(s32[64,12]{0,1:T(8,128)} %param.14) | data formatting | bytes 6144 | tf_op args[3]
  1.4 38.4 %exchange.1 = (f32[3,128,16,128]{3,2,1,0:T(8,128)}, f32[2,32,4,256]{3,2,1,0:T(4,128)}, f32[2,32,16,256]{3,2,1,0:T(8,128)}) custom-call(f32[64,4,256]{2,1,0:T(4,128)} %geometry.3, f32[64,16,256]{2,1,0:T(8,128)} %charges.3, f32[64,16,256]{2,1,0:T(8,128)} %charges.3, f32[64,32,256]{2,1,0:T(8,128)} %basis_far.1, f32[8,8,32,32]{3,2,1,0:T(8,128)} %leaf_transfer_far.1, ...), custom_call_target="tpu_custom_call" | custom-call | tf_op jit(solution)/shard_map/exchange/pallas_call | solution.py:164
  39.8 38.3 %local_part.1 = f32[64,16,256]{2,1,0:T(8,128)} custom-call(s32[64,12]{1,0:T(8,128)} %copy.12.near_list, s32[64]{0:T(128)} %near_count.1, s32[8,16]{1,0:T(8,128)} %box_far_list.1, s32[1,16]{1,0:T(1,128)} %top_far_list.1, f32[64,4,256]{2,1,0:T(4,128)} %geometry.3, f32[2,32,4,256]{3,2,1,0:T(4,128)} %get-tuple-element.8.geo_halo, f32[64,16,256]{2,1,0:T(8,128)} %charges.3, ...), custom_call_target="tpu_custom_call" | custom-call | tf_op jit(solution)/shard_map/local_part/pallas_call | solution.py:361

commit v4 on v3

--- a/solution.py
+++ b/solution.py
@@ -57,6 +57,10 @@
 ORDERS = ((0, 1, 2), (1, 2, 0), (2, 0, 1))
 
 
+OWN_BLOCKS = (8, 0, 24, 24, 8)
+HALO_PIECES = (0, 0, 0, 0, 1, 1, 1, 1)
+
+
 def coordinates(device):
     return (device >> 5, (device >> 1) & 3, (device >> 3) & 3), device & 1
 
@@ -67,8 +71,8 @@
 
 
 def exchange_kernel(
-    geometry, charges_far, charges, basis, leaf_transfer, box_transfer,
-    gathered, geo_halo, ch_halo, moments, send, receive, halo_send, halo_receive,
+    geometry_far, charges_far, geometry, charges, basis, leaf_transfer, box_transfer,
+    gathered, geo_halo, ch_halo, partial, moments, send, receive, halo_send, halo_receive,
 ):
     me = lax.axis_index("group") * 32 + lax.axis_index("dev")
     chip, core = coordinates(me)
@@ -76,19 +80,25 @@
     def device(chip, core):
         return (chip[0], (chip[2] * 4 + chip[1]) * 2 + core)
 
-    def peer(axis, step):
+    def peer(*moves):
         moved = list(chip)
-        moved[axis] = (chip[axis] + step) % 4
+        for axis, step in moves:
+            moved[axis] = (chip[axis] + step) & 3
         return device(moved, core)
 
     sibling = device(chip, 1 - core)
-    above = (me + 1) % 128
-    below = (me + 127) % 128
-    above = (above // 32, above % 32)
-    below = (below // 32, below % 32)
+    above = (me + 1) & 127
+    below = (me + 127) & 127
+    above = (above >> 5, above & 31)
+    below = (below >> 5, below & 31)
+    steps = [(one, two) for one in range(4) for two in range(4) if one or two]
+    partners = [peer((axis, step)) for axis in range(3) for step in (1, 2, 3)]
+    partners += [
+        peer((first, one), (second, two)) for first, second, _ in ORDERS for one in (1, 2, 3) for two in (1, 2, 3)
+    ]
+    partners += [sibling, above, below]
 
     barrier = pltpu.get_barrier_semaphore()
-    partners = [peer(axis, step) for axis in range(3) for step in (1, 2, 3)] + [sibling, above, below]
     for partner in partners:
         pl.semaphore_signal(barrier, inc=1, device_id=partner, device_id_type=pl.DeviceIdType.MESH)
 
@@ -104,17 +114,49 @@
         moments[box] = dot3(jnp.concatenate(parts, axis=1), transfer, NN)
         return carry
 
-    box_moments(0, 0)
+    def own_block(n, carry):
+        here = geometry[n]
+        hi, lo = halves(charges[n] * (here[3:4] * (1.0 / FOUR_PI)))
+        both = jnp.concatenate([hi, lo], axis=0)
+        columns = here.T
+        total = jnp.zeros((RHS, LEAF), f32)
+        for q in range(0, LEAF, 128):
+            squared = jnp.full((128, LEAF), SOFTENING, f32)
+            for comp in range(3):
+                apart = columns[q : q + 128, comp : comp + 1] - here[comp : comp + 1]
+                squared = squared + apart * apart
+            hi, lo = halves(lax.rsqrt(squared))
+            r = dot(both[:, q : q + 128], hi, NN)
+            total = total + (r[:RHS] + r[RHS:] + dot(both[:RHS, q : q + 128], lo, NN))
+        partial[n] = total
+        return carry
+
+    def own_blocks(point):
+        first = sum(OWN_BLOCKS[:point])
+        if OWN_BLOCKS[point]:
+            lax.fori_loop(first, first + OWN_BLOCKS[point], own_block, 0, unroll=4)
+
+    own_blocks(0)
     pl.semaphore_wait(barrier, len(partners))
-    halo = [
-        remote(geometry.at[pl.ds(OWN - REACH, REACH)], geo_halo.at[0], halo_send.at[0], halo_receive.at[0], above),
-        remote(geometry.at[pl.ds(0, REACH)], geo_halo.at[1], halo_send.at[1], halo_receive.at[1], below),
-        remote(charges_far.at[pl.ds(OWN - REACH, REACH)], ch_halo.at[0], halo_send.at[2], halo_receive.at[2], above),
-        remote(charges_far.at[pl.ds(0, REACH)], ch_halo.at[1], halo_send.at[3], halo_receive.at[3], below),
-    ]
-    for copy in halo:
-        copy.start()
-    lax.fori_loop(1, 8, box_moments, 0)
+    halo = []
+
+    def start_halo(source, target, first, count, slot):
+        for side, (begin, partner) in enumerate(((OWN - REACH, above), (0, below))):
+            copy = remote(
+                source.at[pl.ds(begin + first, count)], target.at[side, pl.ds(first, count)],
+                halo_send.at[side, slot], halo_receive.at[side, slot], partner,
+            )
+            copy.start()
+            halo.append(copy)
+
+    def start_pieces(n):
+        for piece in range(len(HALO_PIECES)):
+            if HALO_PIECES[piece] == n:
+                start_halo(charges_far, ch_halo, 4 * piece, 4, piece)
+
+    start_halo(geometry_far, geo_halo, 0, REACH, 8)
+    start_pieces(0)
+    lax.fori_loop(0, 8, box_moments, 0)
     boxes = jnp.concatenate([moments[b] for b in range(8)], axis=1)
     top = dot3(boxes, box_transfer[...].reshape(8 * RANK, RANK), NN)
     own = [row_in(part, chip, core) for part in range(3)]
@@ -122,39 +164,45 @@
     gathered[1, own[1]] = boxes[:, 128:]
     gathered[2, own[2]] = jnp.concatenate([top, jnp.zeros((RHS, 128 - RANK), f32)], axis=1)
 
-    everything = list(halo)
-    waiting = []
-    for stage in range(3):
-        size = 4**stage
-        running = []
-        for part in range(3):
-            axis = ORDERS[part][stage]
-            first = (own[part] // size) * size
-            block = gathered.at[part, pl.ds(first, size)]
-            for step in (1, 2, 3):
-                slot = 3 * stage + step - 1
-                copy = remote(block, block, send.at[part, slot], receive.at[part, slot], peer(axis, step))
-                copy.start()
-                running.append((part, step, copy))
-            if stage == 2:
-                copy = remote(block, block, send.at[part, 9], receive.at[part, 9], sibling)
-                copy.start()
-                waiting.append(copy)
-        for part, step, copy in running:
-            copy.wait_recv()
-            if stage == 2:
-                axis = ORDERS[part][2]
-                third = (chip[axis] + 4 - step) % 4
-                block = gathered.at[part, pl.ds((core * 4 + third) * 16, 16)]
-                forward = remote(block, block, send.at[part, 9 + step], receive.at[part, 9 + step], sibling)
-                forward.start()
-                waiting.append(forward)
-            everything.append(copy)
-    for copy in waiting:
+    planes = []
+    for part in range(3):
+        first, second, _ = ORDERS[part]
+        block = gathered.at[part, own[part]]
+        for slot, (one, two) in enumerate(steps):
+            copy = remote(block, block, send.at[part, slot], receive.at[part, slot], peer((first, one), (second, two)))
+            copy.start()
+            planes.append((part, copy))
+    start_pieces(1)
+    own_blocks(2)
+    lines = []
+    siblings = []
+    for part in range(3):
+        for of, copy in planes:
+            if of == part:
+                copy.wait_recv()
+        third = ORDERS[part][2]
+        block = gathered.at[part, pl.ds((core * 4 + chip[third]) * 16, 16)]
+        for step in (1, 3, 2):
+            slot = 14 + step
+            copy = remote(block, block, send.at[part, slot], receive.at[part, slot], peer((third, step)))
+            copy.start()
+            lines.append((part, step, copy))
+        copy = remote(block, block, send.at[part, 18], receive.at[part, 18], sibling)
+        copy.start()
+        siblings.append(copy)
+    start_pieces(2)
+    own_blocks(3)
+    for part, step, copy in lines:
         copy.wait_recv()
-    for copy in halo:
+        line = (chip[ORDERS[part][2]] + 4 - step) & 3
+        block = gathered.at[part, pl.ds((core * 4 + line) * 16, 16)]
+        forward = remote(block, block, send.at[part, 18 + step], receive.at[part, 18 + step], sibling)
+        forward.start()
+        siblings.append(forward)
+    own_blocks(4)
+    for copy in siblings + halo:
         copy.wait_recv()
-    for copy in everything + waiting:
+    for copy in [copy for _, copy in planes] + [copy for _, _, copy in lines] + siblings + halo:
         copy.wait_send()
 
 
@@ -167,25 +215,26 @@
             jax.ShapeDtypeStruct((3, 128, RHS, 128), f32),
             jax.ShapeDtypeStruct((2, REACH, 4, LEAF), f32),
             jax.ShapeDtypeStruct((2, REACH, RHS, LEAF), f32),
+            jax.ShapeDtypeStruct((OWN, RHS, LEAF), f32),
         ),
-        in_specs=[far, far, vmem, vmem, vmem, vmem],
-        out_specs=(vmem, far, far),
+        in_specs=[far, far, vmem, vmem, vmem, vmem, vmem],
+        out_specs=(vmem, far, far, vmem),
         scratch_shapes=[
             pltpu.VMEM((8, RHS, RANK), f32),
-            pltpu.SemaphoreType.DMA((3, 13)),
-            pltpu.SemaphoreType.DMA((3, 13)),
-            pltpu.SemaphoreType.DMA((4,)),
-            pltpu.SemaphoreType.DMA((4,)),
+            pltpu.SemaphoreType.DMA((3, 22)),
+            pltpu.SemaphoreType.DMA((3, 22)),
+            pltpu.SemaphoreType.DMA((2, 9)),
+            pltpu.SemaphoreType.DMA((2, 9)),
         ],
         compiler_params=pltpu.CompilerParams(vmem_limit_bytes=VMEM, collective_id=0, has_side_effects=True),
         name="exchange",
-    )(geometry, charges, charges, basis, leaf_transfer, box_transfer)
+    )(geometry, charges, geometry, charges, basis, leaf_transfer, box_transfer)
 
 
 def local_kernel(
-    near_list, near_count, box_far_list, top_far_list, geometry, geo_halo, charges, ch_halo,
+    near_list, near_count, box_far_list, top_far_list, geometry, geo_halo, charges, ch_halo, partial,
     gathered_far, top_coupling_far, box_transfer_far, box_coupling_far, leaf_transfer_far, basis_far,
-    out, geo, source, source_rows, target_rows, block_hi, block_lo, total, extent,
+    out, geo, source, source_rows, target_rows, block_hi, block_lo, total, extent, following,
     gathered, top_coupling, box_transfer, box_coupling, leaf_transfer, basis, arrived,
 ):
     loads = [
@@ -226,7 +275,7 @@
         norm = squared_norm(v)
         a, b, c = thirds(jnp.concatenate([v[0:3], one, norm + SOFTENING, rest], axis=0))
         target_rows[n] = jnp.concatenate([a, a, b, b, a, c], axis=0).astype(bf16)
-        total[n] = jnp.zeros((RHS, LEAF), f32)
+        total[n] = partial[n]
         return jnp.maximum(largest, norm)
 
     def neighbour(n, largest):
@@ -247,12 +296,20 @@
 
     @pl.when(compact)
     def _():
-        pairs = lax.fori_loop(0, OWN, lambda n, s: s + near_count[n], 0)
+        pairs = lax.fori_loop(0, OWN, lambda n, s: s + near_count[n] - 1, 0)
 
         def after(leaf, slot):
             row = jnp.minimum(leaf, OWN - 1)
             more = slot + 1 < near_count[row]
-            return jnp.where(more, leaf, jnp.minimum(leaf + 1, OWN)), jnp.where(more, slot + 1, 0)
+            return jnp.where(more, leaf, following[leaf]), jnp.where(more, slot + 1, 1)
+
+        def back(n, next_leaf):
+            leaf = OWN - 1 - n
+            following[leaf] = next_leaf
+            return jnp.where(near_count[leaf] > 1, leaf, next_leaf)
+
+        following[OWN] = jnp.int32(OWN)
+        first = lax.fori_loop(0, OWN, back, jnp.int32(OWN))
 
         def fill(u, leaf, slot):
             row = jnp.minimum(leaf, OWN - 1)
@@ -279,7 +336,7 @@
                 leaf, slot = after(leaf, slot)
             return (leaf, slot, *new)
 
-        start = round_of((jnp.int32(0), jnp.int32(0)), False)
+        start = round_of((first, jnp.int32(1)), False)
         lax.fori_loop(0, (pairs + UNROLL - 1) // UNROLL, lambda t, s: round_of(s, True), start)
 
     @pl.when(jnp.logical_not(compact))
@@ -302,7 +359,7 @@
                     parts.append(r[:RHS] + r[RHS:] + dot(both[:RHS], lo, NT))
                 return running + jnp.concatenate(parts, axis=1)
 
-            total[n] = lax.fori_loop(0, near_count[n], slot_sum, jnp.zeros((RHS, LEAF), f32))
+            total[n] = lax.fori_loop(1, near_count[n], slot_sum, partial[n])
             return carry
 
         lax.fori_loop(0, OWN, leaf_sum, 0)
@@ -361,7 +418,7 @@
     return pl.pallas_call(
         local_kernel,
         out_shape=jax.ShapeDtypeStruct((OWN, RHS, LEAF), f32),
-        in_specs=[smem] * 4 + [vmem] * 4 + [far] * 6,
+        in_specs=[smem] * 4 + [vmem] * 5 + [far] * 6,
         out_specs=vmem,
         scratch_shapes=[
             pltpu.VMEM((WIDE, 4, LEAF), f32),
@@ -372,8 +429,9 @@
             pltpu.VMEM((UNROLL, LEAF, LEAF), bf16),
             pltpu.VMEM((OWN + 1, RHS, LEAF), f32),
             pltpu.SMEM((1,), f32),
+            pltpu.SMEM((OWN + 1,), jnp.int32),
         ]
-        + [pltpu.VMEM(array.shape, f32) for array in arrays[8:]]
+        + [pltpu.VMEM(array.shape, f32) for array in arrays[9:]]
         + [pltpu.SemaphoreType.DMA((6,))],
         compiler_params=pltpu.CompilerParams(vmem_limit_bytes=VMEM),
         name="local_part",
@@ -393,9 +451,9 @@
     top_far_list,
     top_coupling,
 ):
-    gathered, geo_halo, ch_halo = exchange(geometry, charges, leaf_cluster_basis, leaf_transfer, box_transfer)
+    gathered, geo_halo, ch_halo, partial = exchange(geometry, charges, leaf_cluster_basis, leaf_transfer, box_transfer)
     return local_part(
-        near_list, near_count, box_far_list, top_far_list, geometry, geo_halo, charges, ch_halo,
+        near_list, near_count, box_far_list, top_far_list, geometry, geo_halo, charges, ch_halo, partial,
         gathered, top_coupling, box_transfer, box_coupling, leaf_transfer, leaf_cluster_basis,
     )
 

time: 79.3 us -> 74.7 us (0.942)
  the two profiles are of different devices: /device:TPU:1 before, /device:TPU:98 now
where the time goes in v4:
time: 74.7 us; the launch traced here: 74.5 us
  Pallas kernels  73.1 us (98%)
  local copies, waits for them, and re-layouts  1.4 us (2%)
    pallas_call x1, Pallas kernels, local_part(): pl.pallas_call(local_kernel, out_shape=jax.ShapeDtypeStruct((OWN, RHS, LE...  41.1 us
    pallas_call x1, Pallas kernels, exchange(): pl.pallas_call(exchange_kernel, out_shape=(jax.ShapeDtypeStruct((3, 128,...  32 us

profile of v4, /device:TPU:98, one launch (start us, length us, event | category | flops | bytes accessed | tf_op | source)
XLA Modules:
  0.0 74.5 jit_solution(18425247175710444617)
XLA Ops:
  0.0 1.4 %copy.12.near_list = s32[64,12]{1,0:T(8,128)} copy(s32[64,12]{0,1:T(8,128)} %param.14) | data formatting | bytes 6144 | tf_op args[3]
  1.4 32.0 %exchange.1 = (f32[3,128,16,128]{3,2,1,0:T(8,128)}, f32[2,32,4,256]{3,2,1,0:T(4,128)}, f32[2,32,16,256]{3,2,1,0:T(8,128)}, f32[64,16,256]{2,1,0:T(8,128)}) custom-call(f32[64,4,256]{2,1,0:T(4,128)} %geometry.3, f32[64,16,256]{2,1,0:T(8,128)} %charges.3, f32[64,4,256]{2,1,0:T(4,128)} %geometry.3, f32[64,16,256]{2,1,0:T(8,128)} %charges.3, ...), custom_call_target="tpu_custom_call" | custom-call | tf_op jit(solution)/shard_map/exchange/pallas_call | solution.py:212
  33.4 41.1 %local_part.1 = f32[64,16,256]{2,1,0:T(8,128)} custom-call(s32[64,12]{1,0:T(8,128)} %copy.12.near_list, s32[64]{0:T(128)} %near_count.1, s32[8,16]{1,0:T(8,128)} %box_far_list.1, s32[1,16]{1,0:T(1,128)} %top_far_list.1, f32[64,4,256]{2,1,0:T(4,128)} %geometry.3, f32[2,32,4,256]{3,2,1,0:T(4,128)} %get-tuple-element.9.geo_halo, f32[64,16,256]{2,1,0:T(8,128)} %charges.3, ...), custom_call_target="tpu_custom_call" | custom-call | tf_op jit(solution)/shard_map/local_part/pallas_call | solution.py:418

commit v5 on v4

--- a/solution.py
+++ b/solution.py
@@ -58,7 +58,7 @@
 
 
 OWN_BLOCKS = (8, 0, 24, 24, 8)
-HALO_PIECES = (0, 0, 0, 0, 1, 1, 1, 1)
+HALO_PIECES = (0, 0, 0, 1, 1, 1, 1, 1)
 
 
 def coordinates(device):
@@ -71,9 +71,16 @@
 
 
 def exchange_kernel(
-    geometry_far, charges_far, geometry, charges, basis, leaf_transfer, box_transfer,
-    gathered, geo_halo, ch_halo, partial, moments, send, receive, halo_send, halo_receive,
+    geometry_far, charges_far, basis_far, leaf_transfer_far, box_transfer_far, geometry, charges,
+    gathered, geo_halo, ch_halo, partial, moments, basis, leaf_transfer, box_transfer, arrived, send, receive, halo_send, halo_receive,
 ):
+    loads = [
+        pltpu.make_async_copy(basis_far, basis, arrived.at[0]),
+        pltpu.make_async_copy(leaf_transfer_far, leaf_transfer, arrived.at[1]),
+        pltpu.make_async_copy(box_transfer_far, box_transfer, arrived.at[2]),
+    ]
+    for load in loads:
+        load.start()
     me = lax.axis_index("group") * 32 + lax.axis_index("dev")
     chip, core = coordinates(me)
 
@@ -156,6 +163,8 @@
 
     start_halo(geometry_far, geo_halo, 0, REACH, 8)
     start_pieces(0)
+    for load in loads:
+        load.wait()
     lax.fori_loop(0, 8, box_moments, 0)
     boxes = jnp.concatenate([moments[b] for b in range(8)], axis=1)
     top = dot3(boxes, box_transfer[...].reshape(8 * RANK, RANK), NN)
@@ -217,10 +226,14 @@
             jax.ShapeDtypeStruct((2, REACH, RHS, LEAF), f32),
             jax.ShapeDtypeStruct((OWN, RHS, LEAF), f32),
         ),
-        in_specs=[far, far, vmem, vmem, vmem, vmem, vmem],
+        in_specs=[far] * 5 + [vmem] * 2,
         out_specs=(vmem, far, far, vmem),
         scratch_shapes=[
             pltpu.VMEM((8, RHS, RANK), f32),
+            pltpu.VMEM(basis.shape, f32),
+            pltpu.VMEM(leaf_transfer.shape, f32),
+            pltpu.VMEM(box_transfer.shape, f32),
+            pltpu.SemaphoreType.DMA((3,)),
             pltpu.SemaphoreType.DMA((3, 22)),
             pltpu.SemaphoreType.DMA((3, 22)),
             pltpu.SemaphoreType.DMA((2, 9)),
@@ -228,14 +241,14 @@
         ],
         compiler_params=pltpu.CompilerParams(vmem_limit_bytes=VMEM, collective_id=0, has_side_effects=True),
         name="exchange",
-    )(geometry, charges, geometry, charges, basis, leaf_transfer, box_transfer)
+    )(geometry, charges, basis, leaf_transfer, box_transfer, geometry, charges)
 
 
 def local_kernel(
-    near_list, near_count, box_far_list, top_far_list, geometry, geo_halo, charges, ch_halo, partial,
+    near_list_far, near_count, box_far_list, top_far_list, geometry, geo_halo, charges_far, ch_halo_far, partial,
     gathered_far, top_coupling_far, box_transfer_far, box_coupling_far, leaf_transfer_far, basis_far,
     out, geo, source, source_rows, target_rows, block_hi, block_lo, total, extent, following,
-    gathered, top_coupling, box_transfer, box_coupling, leaf_transfer, basis, arrived,
+    gathered, top_coupling, box_transfer, box_coupling, leaf_transfer, basis, charges, ch_halo, near_list, arrived,
 ):
     loads = [
         pltpu.make_async_copy(far, here, arrived.at[n])
@@ -244,7 +257,13 @@
             (box_coupling_far, box_coupling), (leaf_transfer_far, leaf_transfer), (basis_far, basis),
         ))
     ]
-    for load in loads:
+    early = [
+        pltpu.make_async_copy(charges_far, charges, arrived.at[6]),
+        pltpu.make_async_copy(ch_halo_far, ch_halo, arrived.at[7]),
+        pltpu.make_async_copy(near_list_far, near_list, arrived.at[9]),
+        pltpu.make_async_copy(partial, total.at[pl.ds(0, OWN)], arrived.at[8]),
+    ]
+    for load in early + loads:
         load.start()
     offset = lax.axis_index(AXES) * OWN - REACH
     geo[0:REACH] = geo_halo[0]
@@ -266,16 +285,12 @@
 
         lax.fori_loop(0, part.shape[0], leaf, 0, unroll=8)
 
-    weigh(ch_halo.at[0], 0)
-    weigh(charges, REACH)
-    weigh(ch_halo.at[1], REACH + OWN)
 
     def target(n, largest):
         v = geo[n + REACH] - centre
         norm = squared_norm(v)
         a, b, c = thirds(jnp.concatenate([v[0:3], one, norm + SOFTENING, rest], axis=0))
         target_rows[n] = jnp.concatenate([a, a, b, b, a, c], axis=0).astype(bf16)
-        total[n] = partial[n]
         return jnp.maximum(largest, norm)
 
     def neighbour(n, largest):
@@ -289,7 +304,12 @@
 
     nothing = jnp.zeros((1, LEAF), f32)
     targets = lax.fori_loop(0, OWN, target, nothing, unroll=8)
-    sources = lax.fori_loop(0, WIDE, neighbour, nothing, unroll=8)
+    sources = lax.fori_loop(0, WIDE, neighbour, nothing, unroll=16)
+    for load in early:
+        load.wait()
+    weigh(ch_halo.at[0], 0)
+    weigh(charges, REACH)
+    weigh(ch_halo.at[1], REACH + OWN)
     total[OWN] = jnp.zeros((RHS, LEAF), f32)
     extent[0] = jnp.max(targets) + jnp.max(sources)
     compact = extent[0] <= EXTENT
@@ -359,7 +379,7 @@
                     parts.append(r[:RHS] + r[RHS:] + dot(both[:RHS], lo, NT))
                 return running + jnp.concatenate(parts, axis=1)
 
-            total[n] = lax.fori_loop(1, near_count[n], slot_sum, partial[n])
+            total[n] = lax.fori_loop(1, near_count[n], slot_sum, total[n])
             return carry
 
         lax.fori_loop(0, OWN, leaf_sum, 0)
@@ -418,7 +438,7 @@
     return pl.pallas_call(
         local_kernel,
         out_shape=jax.ShapeDtypeStruct((OWN, RHS, LEAF), f32),
-        in_specs=[smem] * 4 + [vmem] * 5 + [far] * 6,
+        in_specs=[far] + [smem] * 3 + [vmem] * 2 + [far] * 9,
         out_specs=vmem,
         scratch_shapes=[
             pltpu.VMEM((WIDE, 4, LEAF), f32),
@@ -432,7 +452,9 @@
             pltpu.SMEM((OWN + 1,), jnp.int32),
         ]
         + [pltpu.VMEM(array.shape, f32) for array in arrays[9:]]
-        + [pltpu.SemaphoreType.DMA((6,))],
+        + [pltpu.VMEM(arrays[n].shape, f32) for n in (6, 7)]
+        + [pltpu.SMEM((OWN, NEAR), jnp.int32)]
+        + [pltpu.SemaphoreType.DMA((10,))],
         compiler_params=pltpu.CompilerParams(vmem_limit_bytes=VMEM),
         name="local_part",
     )(*arrays)

time: 74.7 us -> 70.9 us (0.949)
  the two profiles are of different devices: /device:TPU:98 before, /device:TPU:63 now
where the time goes in v5:
time: 70.9 us; the launch traced here: 70.7 us
  Pallas kernels  69.3 us (98%)
  local copies, waits for them, and re-layouts  1.4 us (2%)
    pallas_call x1, Pallas kernels, local_part(): pl.pallas_call(local_kernel, out_shape=jax.ShapeDtypeStruct((OWN, RHS, LE...  36.5 us
    pallas_call x1, Pallas kernels, exchange(): pl.pallas_call(exchange_kernel, out_shape=(jax.ShapeDtypeStruct((3, 128,...  32.8 us

profile of v5, /device:TPU:63, one launch (start us, length us, event | category | flops | bytes accessed | tf_op | source)
XLA Modules:
  0.0 70.7 jit_solution(8531458358382895827)
XLA Ops:
  0.0 1.4 %copy.12.near_list_far = s32[64,12]{1,0:T(8,128)} copy(s32[64,12]{0,1:T(8,128)} %param.14) | data formatting | bytes 6144 | tf_op args[3]
  1.4 32.8 %exchange.1 = (f32[3,128,16,128]{3,2,1,0:T(8,128)}, f32[2,32,4,256]{3,2,1,0:T(4,128)}, f32[2,32,16,256]{3,2,1,0:T(8,128)}, f32[64,16,256]{2,1,0:T(8,128)}) custom-call(f32[64,4,256]{2,1,0:T(4,128)} %geometry.3, f32[64,16,256]{2,1,0:T(8,128)} %charges_far.3, f32[64,32,256]{2,1,0:T(8,128)} %basis_far.3, f32[8,8,32,32]{3,2,1,0:T(8,128)} %leaf_transfer_far.3, ...), custom_call_target="tpu_custom_call" | custom-call | tf_op jit(solution)/shard_map/exchange/pallas_call | solution.py:221
  34.2 36.5 %local_part.1 = f32[64,16,256]{2,1,0:T(8,128)} custom-call(s32[64,12]{1,0:T(8,128)} %copy.12.near_list_far, s32[64]{0:T(128)} %near_count.1, s32[8,16]{1,0:T(8,128)} %box_far_list.1, s32[1,16]{1,0:T(1,128)} %top_far_list.1, f32[64,4,256]{2,1,0:T(4,128)} %geometry.3, f32[2,32,4,256]{3,2,1,0:T(4,128)} %get-tuple-element.9.geo_halo, ...), custom_call_target="tpu_custom_call" | custom-call | tf_op jit(solution)/shard_map/local_part/pallas_call | solution.py:438
